TPU v7x, 32 devices: a whole 2x2x4 slice. The times are simulated.
32 devices in a mesh: groups: 2 (over x), stream: 16 (over z, y, core).
Axes of the slice: x: 2, y: 2, z: 4, core: 2. Of those that a mesh axis runs over, the one named last changes fastest.
Arguments:
- hidden_units: bfloat16 [64, 3584], P('groups', 'stream'), parts along dimension 0, may hold values from -6 to 6
- residual: bfloat16 [64, 8192], P(('groups', 'stream')), parts along dimension 0, may hold values from -6 to 6
- down_weight: bfloat16 [3584, 8192], P('stream'), may hold values from -0.09375 to 0.09375
- final_gain: bfloat16 [8192], replicated, may hold values from 0.5 to 1.5
- head_weight: bfloat16 [8192, 8192], P('stream'), may hold values from -0.19824219 to 0.19824219
- targets: int32 [64], P('groups'), parts along dimension 0, may hold values from 0 to 8191
- segments: int32 [64], P(('groups', 'stream')), parts along dimension 0, may hold values from 1 to 4, as said below
- train_loss: float32 [64], P(('groups', 'stream')), parts along dimension 0, may hold values from 12 to 20
Outputs:
- hidden_states: bfloat16 [64, 8192], P(('groups', 'stream')), parts along dimension 0
- loss_weight: float32 [64], P(('groups', 'stream')), parts along dimension 0
There are 2 independent parts, one for each index of `groups`. A program takes and returns all parts, laid end to end along the dimension named above; an argument that names none is the same for every part. Nothing has to cross between parts.
Inputs may be any that keep to these rules, and one draw needn't show every extreme that they name: `segments`: document numbers start at 1 and rise by one at each new document; the first document holds exactly the first 16 tokens; every later aligned block of 16 tokens begins a document at its first token and begins exactly two more inside it, so each document holds 1 to 16 consecutive tokens.
All inputs are finite; a program needn't handle non-finite values.
Results may differ from a plain program's by a relative error of at most 0.0083.
Values may be sent and summed in bfloat16 or wider, within the bound.
No kernel may reach another device: no remote copies, remote signals or barrier semaphores. Data moves between devices by JAX's collectives and lax.ppermute only.
A program may use at most 128 MiB of HBM per device.

v0:
```python
import jax
import jax.numpy as jnp
from jax import lax
from jax.sharding import PartitionSpec as P


def passed_along(block, axis, distance):
    devices = range(lax.axis_size(axis))
    route = [(i - distance, i) for i in devices if i - distance in devices]
    return lax.ppermute(block, axis, route)


def normalize(states, final_gain):
    values = states.astype(jnp.float32)
    mean_sq = jnp.mean(values * values, axis=-1, keepdims=True)
    return (values * lax.rsqrt(mean_sq + 1e-05) * final_gain.astype(jnp.float32)).astype(
        jnp.bfloat16
    )


def vocab_terms(rows, head_weight, row_targets, vocab_start):
    logits = jnp.einsum("td,vd->tv", rows, head_weight, preferred_element_type=jnp.float32)
    sum_exp = jnp.sum(jnp.exp(logits), axis=1)
    vocab_ids = vocab_start + lax.broadcasted_iota(jnp.int32, logits.shape, 1)
    matches = row_targets[:, None] == vocab_ids
    target_logit = jnp.sum(jnp.where(matches, logits, 0.0), axis=1)
    return (sum_exp, target_logit)


def on_device(
    hidden_units, residual, down_weight, final_gain, head_weight, targets, segments, train_loss
):
    tok_rows = residual.shape[0]
    vocab_rows = head_weight.shape[0]
    device_index = lax.axis_index("stream")
    vocab_start = device_index * vocab_rows
    summed = lax.psum(
        jnp.dot(hidden_units, down_weight, preferred_element_type=jnp.float32), "stream"
    )
    all_rows = lax.all_gather(residual, "stream", axis=0, tiled=True)
    states_all = (all_rows.astype(jnp.float32) + summed).astype(jnp.bfloat16)
    hidden_states = lax.dynamic_slice_in_dim(states_all, device_index * tok_rows, tok_rows, 0)
    normed_all = normalize(states_all, final_gain)
    sum_exp, target_logit = vocab_terms(normed_all, head_weight, targets, vocab_start)
    own_exp, own_target = (
        lax.psum_scatter(sum_exp, "stream", scatter_dimension=0, tiled=True),
        lax.psum_scatter(target_logit, "stream", scatter_dimension=0, tiled=True),
    )
    ref_loss = jnp.log(own_exp) - own_target
    next_first = passed_along(segments[:1], "stream", -1)
    next_ids = jnp.concatenate([segments[1:], next_first])
    positions = device_index * tok_rows + lax.broadcasted_iota(jnp.int32, (tok_rows,), 0)
    inside = positions + 1 < tok_rows * lax.axis_size("stream")
    same_doc = jnp.where(inside & (next_ids == segments), 1.0, 0.0).astype(jnp.float32)
    loss_weight = same_doc * jax.nn.sigmoid(train_loss - ref_loss)
    return (hidden_states, loss_weight)


def solution(mesh):
    placed = (
        P("groups", "stream"),
        P(("groups", "stream"), None),
        P("stream", None),
        P(),
        P("stream", None),
        P("groups"),
        P(("groups", "stream")),
        P(("groups", "stream")),
    )
    return jax.shard_map(
        on_device,
        mesh=mesh,
        in_specs=placed,
        out_specs=(P(("groups", "stream"), None), P(("groups", "stream"))),
        check_vma=False,
    )
```

profile of v0, /device:TPU:0, one launch (start us, length us, event | category | flops | bytes accessed | tf_op | source)
XLA Modules:
  0.0 156.2 jit_solution(5379465729068068778)
XLA Ops:
  7.2 0.0 copy-start
  7.2 0.0 copy-start.2
  7.2 0.0 all-reduce.5.cloned.1.call-start
  7.2 0.7 copy-done
  7.9 3.8 %fusion.9 = f32[32,8192]{1,0:T(8,128)} fusion(bf16[32,224]{1,0:T(8,128)(2,1)S(1)} %copy-done, bf16[224,8192]{1,0:T(8,128)(2,1)} %param.10), kind=kOutput, calls=%fused_computation.20 | convolution fusion | flops 117440512 | bytes 4732928 | tf_op jit(solution)/shard_map/dot_general | solution.py:38
  11.7 0.0 copy-start.1
  11.7 0.0 copy-start.3
  11.7 0.0 all-reduce.5.cloned.1.call-update
  11.8 1.3 fusion.8
  13.1 1.3 collective-permute-start
  14.4 26.2 %all-gather = bf16[16,2,8192]{2,1,0:T(2,128)(2,1)S(1)} all-gather(bf16[1,2,8192]{2,1,0:T(2,128)(2,1)} %bitcast.5), channel_id=1, replica_groups=mesh['groups'=2,'stream'=16] {'stream'}, dimensions={0}, use_global_device_ids=true | all-gather | bytes 557056 | tf_op jit(solution)/shard_map/all_gather | solution.py:40
  40.5 0.1 reshape.16
  40.7 0.7 convert_element_type.18
  41.4 1.2 dynamic-slice
  43.3 65.4 %all-reduce.5.cloned.1.call-done = f32[32,8192]{1,0:T(8,128)} async-done(((f32[32,8192]{1,0:T(8,128)}), f32[32,8192]{1,0:T(8,128)}) %all-reduce.5.cloned.1.call-update) | async-done | bytes 1048592 | tf_op jit(solution)/shard_map/psum | solution.py:37
  108.7 1.5 fusion
  110.1 0.7 constant_dynamic-slice_fusion
  110.8 0.0 copy-done.2
  110.8 6.1 %exponential_reduce_fusion = (f32[32]{0:T(128)S(1)}, f32[32]{0:T(128)S(1)}) fusion(s32[512]{0:T(512)S(1)} %iota_add_fusion, s32[32]{0:T(128)S(1)} %copy-done.2, bf16[512,8192]{1,0:T(8,128)(2,1)} %param.12, bf16[32,8192]{1,0:T(8,128)(2,1)S(1)} %get-tuple-element.7, f32[8192]{0:T(1024)S(1)} %convert_element_type.18, f32[32]{0:T(128)S(1)} %add_rsqrt_fusion), kind=kOutput, calls=%fused_computation.10 | convolution fusion | flops 269549504 | bytes 8948224 | tf_op jit(solution)/shard_map/td,vd->tv/dot_general | solution.py:22
  116.9 30.6 %all-reduce.2 = (f32[32]{0:T(128)S(1)}, f32[32]{0:T(128)S(1)}) all-reduce(f32[32]{0:T(128)S(1)} %get-tuple-element.3, f32[32]{0:T(128)S(1)} %get-tuple-element.2), channel_id=3, replica_groups=mesh['groups'=2,'stream'=16] {'stream'}, use_global_device_ids=true, to_apply=%region_5.6.clone | all-reduce | flops 64 | bytes 512
  147.5 0.0 collective-permute-done
  147.6 0.0 copy-done.1
  147.6 0.0 copy-done.3
  147.6 1.8 %divide_multiply_fusion = f32[2]{0:T(128)} fusion(s32[2]{0:T(128)S(1)} %copy-done.1, s32[1]{0:T(128)} %collective-permute-done, s32[1]{0:T(128)} %get-tuple-element.8, f32[2]{0:T(128)S(1)} %copy-done.3, f32[32]{0:T(128)S(1)} %get-tuple-element.4, u32[]{:T(128)S(6)} %multiply.7, f32[32]{0:T(128)S(1)} %get-tuple-element.5, s32[]{:T(128)S(6)} %mul.29), kind=kLoop, calls=%fused_computation.13 | loop fusion | flops 26 | bytes 56 | tf_op jit(solution)/shard_map/mul | solution.py:55
  (2 shorter events, 0.0 us)
Async XLA Ops:
  7.2 0.7 copy-start
  7.2 103.6 %copy-start.2 = (s32[32]{0:T(128)S(1)}, s32[32]{0:T(128)}, u32[]{:S(2)}) copy-start(s32[32]{0:T(128)} %param.13) | copy-start | bytes 388
  7.2 101.5 %all-reduce.5.cloned.1.call-start = ((), (), s32[]{:S(2)}) async-start(), calls=%async_computation | async-start | bytes 2097152 | tf_op jit(solution)/shard_map/psum | solution.py:37
  11.7 135.8 %copy-start.1 = (s32[2]{0:T(128)S(1)}, s32[2]{0:T(128)}, u32[]{:S(2)}) copy-start(s32[2]{0:T(128)} %param.14) | copy-start | bytes 28
  11.7 135.8 %copy-start.3 = (f32[2]{0:T(128)S(1)}, f32[2]{0:T(128)}, u32[]{:S(2)}) copy-start(f32[2]{0:T(128)} %param.15) | copy-start | bytes 28
  13.1 134.5 %collective-permute-start = (s32[1]{0:T(128)}, s32[1]{0:T(128)}, u32[]{:S(2)}, u32[]{:S(2)}) collective-permute-start(s32[1]{0:T(128)} %get-tuple-element.9), channel_id=1, source_target_pairs={{1,0},{2,1},{3,2},{4,3},{5,4},{6,5},{7,6},{8,7},{9,8},{10,9},{11,1... | collective-permute-start | bytes 20 | tf_op jit(solution)/shard_map/ppermute | solution.py:10
Sparse Core Ops, SparseCore 0:
  11.9 96.7 all-reduce.4
where the time goes:
time: 157 us; the launch traced here: 156 us
  waiting for transfers between devices  65.4 us (42%)
  blocking collectives  56.8 us (36%)
  between operations  14.7 us (9%)
  matrix products  9.95 us (6%)
  local copies, waits for them, and re-layouts  4.05 us (3%)
  other arithmetic  4.02 us (3%)
    psum x1, waiting for transfers between devices, on_device(): lax.psum(jnp.dot(hidden_units, down_weight, preferred_element_type=jnp.fl...  65.4 us
    unnamed x1, blocking collectives  30.6 us
    all_gather x1, blocking collectives, on_device(): all_rows = lax.all_gather(residual, 'stream', axis=0, tiled=True)  26.2 us
    dot_general x1, matrix products, vocab_terms(): jnp.einsum('td,vd->tv', rows, head_weight, preferred_element_type=jnp.flo...  6.11 us
    dot_general x1, matrix products, on_device(): jnp.dot(hidden_units, down_weight, preferred_element_type=jnp.float32)  3.84 us
  transfers between devices with their start and end apart: 2, of which 1 were waited for; matrix products, arithmetic and copies ran while one was open for 7% of the time, Pallas kernels for 0%

commit v1 on v0

v1 whole, which is shorter than its diff:
```python
import jax
import jax.numpy as jnp
import numpy as np
from jax import lax
from jax.sharding import PartitionSpec as P

AXIS = "stream"
F32 = jnp.float32
BF16 = jnp.bfloat16


def levels_of(devices):
    levels, stride = [(1, 2)], 2
    while stride < devices:
        size = 4 if (devices // stride) % 4 == 0 else 2
        levels.append((stride, size))
        stride *= size
    assert stride == devices
    return levels


def offsets_of(levels):
    offsets = np.zeros((1,), np.int32)
    for stride, size in levels:
        offsets = (offsets[:, None] + stride * np.arange(size, dtype=np.int32)[None, :]).reshape(-1)
    return offsets


def swapped(block, distance):
    return lax.ppermute(block, AXIS, [(i, i ^ distance) for i in range(lax.axis_size(AXIS))])


def fold(block, level):
    stride, size = level
    parts = block.reshape((size, -1) + block.shape[1:])
    came = [swapped(parts[k], stride * k) for k in range(size - 1, 0, -1)]
    return sum(came, parts[0])


def exchange(block, level):
    stride, size = level
    parts = block.reshape((size, -1) + block.shape[1:])
    came = {k: swapped(parts, stride * k) for k in range(size - 1, 0, -1)}
    out = []
    for place in range(size):
        terms = [(k, came[k][place ^ k]) for k in range(1, size)] + [(0, parts[place])]
        out.append(sum((t for _, t in terms[1:]), terms[0][1]))
    return jnp.stack(out).reshape(block.shape)


def spread(block, level):
    stride, size = level
    came = {k: swapped(block, stride * k) for k in range(size - 1, 0, -1)}
    return jnp.concatenate([block] + [came[k] for k in range(1, size)], axis=0)


def on_device(
    hidden_units, residual, down_weight, final_gain, head_weight, targets, segments, train_loss
):
    own = residual.shape[0]
    tokens = hidden_units.shape[0]
    vocab_rows = head_weight.shape[0]
    devices = lax.axis_size(AXIS)
    device_index = lax.axis_index(AXIS)
    levels = levels_of(devices)
    offsets = offsets_of(levels)

    holder = device_index ^ jnp.asarray(offsets)
    places = (holder[:, None] * own + jnp.arange(own, dtype=jnp.int32)[None, :]).reshape(-1)
    chosen = places[:, None] == lax.broadcasted_iota(jnp.int32, (tokens, tokens), 1)
    hidden = jnp.dot(chosen.astype(BF16), hidden_units, preferred_element_type=F32).astype(BF16)
    row_targets = jnp.sum(jnp.where(chosen, targets[None, :], 0), axis=1)

    part = jnp.dot(hidden, down_weight, preferred_element_type=F32)
    for level in levels[:-1]:
        part = fold(part, level)
    part = jnp.concatenate([part[:own] + residual.astype(F32), part[own:]], axis=0)
    states = exchange(part, levels[-1]).astype(BF16)
    hidden_states = states[:own]
    values = states.astype(F32)
    mean_sq = jnp.mean(values * values, axis=-1, keepdims=True)
    normed = (values * lax.rsqrt(mean_sq + 1e-05) * final_gain.astype(F32)).astype(BF16)
    for level in levels[-2::-1]:
        normed = spread(normed, level)

    logits = jnp.einsum("td,vd->tv", normed, head_weight, preferred_element_type=F32)
    sum_exp = jnp.sum(jnp.exp(logits), axis=1)
    vocab_ids = device_index * vocab_rows + lax.broadcasted_iota(jnp.int32, logits.shape, 1)
    target_logit = jnp.sum(jnp.where(row_targets[:, None] == vocab_ids, logits, 0.0), axis=1)
    before_own = places == device_index * own - 1
    next_first = jnp.where(before_own, segments[0].astype(F32), 0.0)
    message = jnp.stack([sum_exp, target_logit, next_first], axis=1)
    for level in levels:
        message = fold(message, level)

    ref_loss = jnp.log(message[:, 0]) - message[:, 1]
    next_ids = jnp.concatenate([segments[1:], message[own - 1 :, 2].astype(jnp.int32)])
    positions = device_index * own + jnp.arange(own, dtype=jnp.int32)
    same_doc = jnp.where((positions + 1 < tokens) & (next_ids == segments), 1.0, 0.0)
    loss_weight = same_doc.astype(F32) * jax.nn.sigmoid(train_loss - ref_loss)
    return (hidden_states, loss_weight)


def solution(mesh):
    placed = (
        P("groups", "stream"),
        P(("groups", "stream"), None),
        P("stream", None),
        P(),
        P("stream", None),
        P("groups"),
        P(("groups", "stream")),
        P(("groups", "stream")),
    )
    return jax.shard_map(
        on_device,
        mesh=mesh,
        in_specs=placed,
        out_specs=(P(("groups", "stream"), None), P(("groups", "stream"))),
        check_vma=False,
    )
```

time: 157 us -> 57.4 us (0.37)
  blocking collectives: 56.8 us -> 0 us
  waiting for transfers between devices: 65.4 us -> 22 us
  starting transfers between devices: 1.32 us -> 17.9 us
  between operations: 14.7 us -> 2.15 us
    psum x1 -> x0, waiting for transfers between devices: 65.4 us -> none  [on_device(): lax.psum(jnp.dot(hidden_units, down_weight, preferred_element_type=jnp.fl...]
    unnamed x1 -> x0, blocking collectives: 30.6 us -> none
    all_gather x1 -> x0, blocking collectives: 26.2 us -> none  [on_device(): all_rows = lax.all_gather(residual, 'stream', axis=0, tiled=True)]
    ppermute x1 -> x14, waiting for transfers between devices: 0.01 us -> 22 us  [swapped(): lax.ppermute(block, AXIS, [(i, i ^ distance) for i in range(lax.axis_size...]
    ppermute x1 -> x14, starting transfers between devices: 1.28 us -> 17.9 us  [swapped(): lax.ppermute(block, AXIS, [(i, i ^ distance) for i in range(lax.axis_size...]
    unnamed x9 -> x12, local copies, waits for them, and re-layouts: 1.91 us -> 0.03 us
  transfers between devices with their start and end apart: 2 -> 14, of which waited for: 1 -> 11; matrix products, arithmetic and copies ran while one was open for 7% -> 3% of each run, Pallas kernels for 0% -> 0%
where the time goes in v1:
time: 57.4 us; the launch traced here: 57.1 us
  waiting for transfers between devices  22 us (38%)
  starting transfers between devices  17.9 us (31%)
  matrix products  9.07 us (16%)
  other arithmetic  3.06 us (5%)
  local copies, waits for them, and re-layouts  2.9 us (5%)
  between operations  2.15 us (4%)
    ppermute x14, waiting for transfers between devices, swapped(): lax.ppermute(block, AXIS, [(i, i ^ distance) for i in range(lax.axis_size...  22 us
    ppermute x14, starting transfers between devices, swapped(): lax.ppermute(block, AXIS, [(i, i ^ distance) for i in range(lax.axis_size...  17.9 us
    dot_general x1, matrix products, on_device(): jnp.einsum('td,vd->tv', normed, head_weight, preferred_element_type=F32)  6.11 us
    dot_general x1, matrix products, on_device(): part = jnp.dot(hidden, down_weight, preferred_element_type=F32)  2.97 us
    mul x1, other arithmetic, on_device(): loss_weight = same_doc.astype(F32) * jax.nn.sigmoid(train_loss - ref_loss)  1.21 us
  transfers between devices with their start and end apart: 14, of which 11 were waited for; matrix products, arithmetic and copies ran while one was open for 3% of the time, Pallas kernels for 0%

profile of v1, /device:TPU:0, one launch (start us, length us, event | category | flops | bytes accessed | tf_op | source)
XLA Modules:
  0.0 57.1 jit_solution(7063322370752295732)
XLA Ops:
  0.7 0.7 %xor_multiply_fusion = s32[16]{0:T(128)S(1)} fusion(s32[16]{0:T(128)} %constant.30.clone, s32[]{:T(128)S(6)} %axis_index.12), kind=kLoop, calls=%fused_computation.33 | loop fusion | flops 32 | bytes 132 | tf_op jit(solution)/shard_map/mul | solution.py:69
  1.5 3.0 %fusion = f32[32,8192]{1,0:T(8,128)S(1)} fusion(bf16[224,8192]{1,0:T(8,128)(2,1)} %param.11, bf16[32,224]{1,0:T(8,128)(2,1)S(1)} %copy-done, s32[32]{0:T(128)S(1)} %add.98), kind=kOutput, calls=%fused_computation.1 | convolution fusion | flops 117907456 | bytes 4733056 | tf_op jit(solution)/shard_map/dot_general | solution.py:74
  4.6 0.5 collective-permute-start
  5.1 1.5 %collective-permute-done = f32[16,8192]{1,0:T(8,128)S(1)} collective-permute-done((f32[16,8192]{1,0:T(8,128)S(1)}, f32[16,8192]{1,0:T(8,128)S(1)}, u32[]{:S(2)}, u32[]{:S(2)}) %collective-permute-start) | collective-permute-done | bytes 524320 | tf_op jit(solution)/shard_map/ppermute | solution.py:30
  6.8 4.0 %collective-permute-start.1 = (f32[4,8192]{1,0:T(4,128)S(1)}, f32[4,8192]{1,0:T(4,128)S(1)}, u32[]{:S(2)}, u32[]{:S(2)}) collective-permute-start(f32[4,8192]{1,0:T(4,128)S(1)} %get-tuple-element.6), channel_id=1, source_target_pairs={{0,6},{1,7},{2,4},{3,5},{4,2},{5,3},{6,0},{7,1},{8,14},{9,15},{10,... | collective-permute-start | bytes 393224 | tf_op jit(solution)/shard_map/ppermute | solution.py:30
  10.7 0.5 collective-permute-start.2
  11.2 0.2 collective-permute-start.3
  11.4 3.6 %collective-permute-done.1 = f32[4,8192]{1,0:T(4,128)S(1)} collective-permute-done((f32[4,8192]{1,0:T(4,128)S(1)}, f32[4,8192]{1,0:T(4,128)S(1)}, u32[]{:S(2)}, u32[]{:S(2)}) %collective-permute-start.1) | collective-permute-done | bytes 131104 | tf_op jit(solution)/shard_map/ppermute | solution.py:30
  15.0 2.5 %collective-permute-done.2 = f32[4,8192]{1,0:T(4,128)S(1)} collective-permute-done((f32[4,8192]{1,0:T(4,128)S(1)}, f32[4,8192]{1,0:T(4,128)S(1)}, u32[]{:S(2)}, u32[]{:S(2)}) %collective-permute-start.2) | collective-permute-done | bytes 131104 | tf_op jit(solution)/shard_map/ppermute | solution.py:30
  17.8 2.6 %collective-permute-start.4 = (f32[2,2,8192]{2,1,0:T(2,128)S(1)}, f32[2,2,8192]{2,1,0:T(2,128)S(1)}, u32[]{:S(2)}, u32[]{:S(2)}) collective-permute-start(f32[2,2,8192]{2,1,0:T(2,128)S(1)} %reshape.120), channel_id=1, source_target_pairs={{0,8},{1,9},{2,10},{3,11},{4,12},{5,13},{6,14},{7,15},{8,0},{9,1},... | collective-permute-start | bytes 393224 | tf_op jit(solution)/shard_map/ppermute | solution.py:30
  20.5 6.1 %collective-permute-done.4 = f32[2,2,8192]{2,1,0:T(2,128)S(1)} collective-permute-done((f32[2,2,8192]{2,1,0:T(2,128)S(1)}, f32[2,2,8192]{2,1,0:T(2,128)S(1)}, u32[]{:S(2)}, u32[]{:S(2)}) %collective-permute-start.4) | collective-permute-done | bytes 131104 | tf_op jit(solution)/shard_map/ppermute | solution.py:30
  26.6 0.2 multiply_reduce_fusion
  27.1 2.0 %collective-permute-start.5 = (bf16[4,8192]{1,0:T(4,128)(2,1)S(1)}, bf16[4,8192]{1,0:T(4,128)(2,1)S(1)}, u32[]{:S(2)}, u32[]{:S(2)}) collective-permute-start(bf16[4,8192]{1,0:T(4,128)(2,1)S(1)} %multiply_convert_fusion), channel_id=1, source_target_pairs={{0,2},{1,3},{2,0},{3,1},{4,6},{5,7},{6,4},{7,5},{8,10},{9,11},{10,... | collective-permute-start | bytes 196616 | tf_op jit(solution)/shard_map/ppermute | solution.py:30
  29.1 0.7 %collective-permute-start.6 = (bf16[4,8192]{1,0:T(4,128)(2,1)S(1)}, bf16[4,8192]{1,0:T(4,128)(2,1)S(1)}, u32[]{:S(2)}, u32[]{:S(2)}) collective-permute-start(bf16[4,8192]{1,0:T(4,128)(2,1)S(1)} %multiply_convert_fusion), channel_id=1, source_target_pairs={{0,4},{1,5},{2,6},{3,7},{4,0},{5,1},{6,2},{7,3},{8,12},{9,13},{10,... | collective-permute-start | bytes 196616 | tf_op jit(solution)/shard_map/ppermute | solution.py:30
  29.8 0.9 %collective-permute-start.7 = (bf16[4,8192]{1,0:T(4,128)(2,1)S(1)}, bf16[4,8192]{1,0:T(4,128)(2,1)S(1)}, u32[]{:S(2)}, u32[]{:S(2)}) collective-permute-start(bf16[4,8192]{1,0:T(4,128)(2,1)S(1)} %multiply_convert_fusion), channel_id=1, source_target_pairs={{0,6},{1,7},{2,4},{3,5},{4,2},{5,3},{6,0},{7,1},{8,14},{9,15},{10,... | collective-permute-start | bytes 196616 | tf_op jit(solution)/shard_map/ppermute | solution.py:30
  30.6 0.6 %fusion.9 = (s32[1]{0:T(128)}, s32[1]{0:T(128)}) fusion(s32[2]{0:T(128)S(1)} %copy-done.3), kind=kLoop, calls=%fused_computation.36 | loop fusion | bytes 16 | tf_op jit(solution)/shard_map/slice | solution.py:97
  32.0 1.4 %collective-permute-done.6 = bf16[4,8192]{1,0:T(4,128)(2,1)S(1)} collective-permute-done((bf16[4,8192]{1,0:T(4,128)(2,1)S(1)}, bf16[4,8192]{1,0:T(4,128)(2,1)S(1)}, u32[]{:S(2)}, u32[]{:S(2)}) %collective-permute-start.6) | collective-permute-done | bytes 65568 | tf_op jit(solution)/shard_map/ppermute | solution.py:30
  33.4 1.6 %collective-permute-done.7 = bf16[4,8192]{1,0:T(4,128)(2,1)S(1)} collective-permute-done((bf16[4,8192]{1,0:T(4,128)(2,1)S(1)}, bf16[4,8192]{1,0:T(4,128)(2,1)S(1)}, u32[]{:S(2)}, u32[]{:S(2)}) %collective-permute-start.7) | collective-permute-done | bytes 65568 | tf_op jit(solution)/shard_map/ppermute | solution.py:30
  35.5 1.2 %collective-permute-done.8 = bf16[16,8192]{1,0:T(8,128)(2,1)S(1)} collective-permute-done((bf16[16,8192]{1,0:T(8,128)(2,1)S(1)}, bf16[16,8192]{1,0:T(8,128)(2,1)S(1)}, u32[]{:S(2)}, u32[]{:S(2)}) %collective-permute-start.8) | collective-permute-done | bytes 262176 | tf_op jit(solution)/shard_map/ppermute | solution.py:30
  36.7 0.3 concatenate.15
  37.0 6.1 %exponential_reduce_fusion = (f32[32]{0:T(128)S(1)}, f32[32]{0:T(128)S(1)}) fusion(s32[512]{0:T(512)S(1)} %iota_add_fusion.1, s32[32]{0:T(128)S(1)} %select_reduce_fusion.1, bf16[32,8192]{1,0:T(8,128)(2,1)S(1)} %concatenate.15, bf16[512,8192]{1,0:T(8,128)(2,1)} %param.13), kind=kOutput, calls=%fused_computation.15 | convolution fusion | flops 268500928 | bytes 8915328 | tf_op jit(solution)/shard_map/td,vd->tv/dot_general | solution.py:86
  43.3 0.6 %slice_bitcast_fusion = bf16[2,8192]{1,0:T(2,128)(2,1)} fusion(bf16[2,2,8192]{2,1,0:T(2,128)(2,1)S(1)} %get-tuple-element.5), kind=kLoop, calls=%fused_computation.16 | loop fusion | bytes 65536 | tf_op jit(solution)/shard_map/slice | solution.py:79
  43.9 0.4 collective-permute-done.9
  44.4 0.9 %collective-permute-start.10 = (f32[4,3]{0,1:T(4,128)S(1)}, f32[4,3]{0,1:T(4,128)S(1)}, u32[]{:S(2)}, u32[]{:S(2)}) collective-permute-start(f32[4,3]{0,1:T(4,128)S(1)} %get-tuple-element.13), channel_id=1, source_target_pairs={{0,6},{1,7},{2,4},{3,5},{4,2},{5,3},{6,0},{7,1},{8,14},{9,15},{10,... | collective-permute-start | bytes 152 | tf_op jit(solution)/shard_map/ppermute | solution.py:30
  45.3 1.2 %collective-permute-start.11 = (f32[4,3]{0,1:T(4,128)S(1)}, f32[4,3]{0,1:T(4,128)S(1)}, u32[]{:S(2)}, u32[]{:S(2)}) collective-permute-start(f32[4,3]{0,1:T(4,128)S(1)} %get-tuple-element.15), channel_id=1, source_target_pairs={{0,4},{1,5},{2,6},{3,7},{4,0},{5,1},{6,2},{7,3},{8,12},{9,13},{10,... | collective-permute-start | bytes 152 | tf_op jit(solution)/shard_map/ppermute | solution.py:30
  46.5 1.4 %collective-permute-start.12 = (f32[4,3]{0,1:T(4,128)S(1)}, f32[4,3]{0,1:T(4,128)S(1)}, u32[]{:S(2)}, u32[]{:S(2)}) collective-permute-start(f32[4,3]{0,1:T(4,128)S(1)} %get-tuple-element.14), channel_id=1, source_target_pairs={{0,2},{1,3},{2,0},{3,1},{4,6},{5,7},{6,4},{7,5},{8,10},{9,11},{10,... | collective-permute-start | bytes 152 | tf_op jit(solution)/shard_map/ppermute | solution.py:30
  47.9 1.0 %collective-permute-done.10 = f32[4,3]{0,1:T(4,128)S(1)} collective-permute-done((f32[4,3]{0,1:T(4,128)S(1)}, f32[4,3]{0,1:T(4,128)S(1)}, u32[]{:S(2)}, u32[]{:S(2)}) %collective-permute-start.10) | collective-permute-done | bytes 80 | tf_op jit(solution)/shard_map/ppermute | solution.py:30
  48.9 1.2 %collective-permute-done.12 = f32[4,3]{0,1:T(4,128)S(1)} collective-permute-done((f32[4,3]{0,1:T(4,128)S(1)}, f32[4,3]{0,1:T(4,128)S(1)}, u32[]{:S(2)}, u32[]{:S(2)}) %collective-permute-start.12) | collective-permute-done | bytes 80 | tf_op jit(solution)/shard_map/ppermute | solution.py:30
  50.1 2.9 %collective-permute-start.13 = (f32[2,3]{0,1:T(4,128)S(1)}, f32[2,3]{0,1:T(4,128)S(1)}, u32[]{:S(2)}, u32[]{:S(2)}) collective-permute-start(f32[2,3]{0,1:T(4,128)S(1)} %slice.114), channel_id=1, source_target_pairs={{0,8},{1,9},{2,10},{3,11},{4,12},{5,13},{6,14},{7,15},{8,0},{9,1},... | collective-permute-start | bytes 80 | tf_op jit(solution)/shard_map/ppermute | solution.py:30
  53.0 1.6 %collective-permute-done.13 = f32[2,3]{0,1:T(4,128)S(1)} collective-permute-done((f32[2,3]{0,1:T(4,128)S(1)}, f32[2,3]{0,1:T(4,128)S(1)}, u32[]{:S(2)}, u32[]{:S(2)}) %collective-permute-start.13) | collective-permute-done | bytes 56 | tf_op jit(solution)/shard_map/ppermute | solution.py:30
  54.6 0.6 %slice.115 = f32[1,1]{0,1:T(1,128)} slice(f32[2,3]{0,1:T(4,128)S(1)} %slice_add_fusion.5), slice={[1:2], [2:3]} | slice | bytes 8 | tf_op jit(solution)/shard_map/slice | solution.py:97
  55.9 1.2 %divide_multiply_fusion = f32[2]{0:T(128)} fusion(f32[2]{0:T(128)S(1)} %copy-done.4, f32[2,3]{0,1:T(4,128)S(1)} %slice_add_fusion.5, s32[2]{0:T(128)S(1)} %copy-done.3, s32[1]{0:T(128)} %bitcast.6, s32[1]{0:T(128)} %get-tuple-element.16, s32[]{:T(128)S(6)} %mul.35), kind=kLoop, calls=%fused_computation.29 | loop fusion | flops 26 | bytes 52 | tf_op jit(solution)/shard_map/mul | solution.py:100
  (44 shorter events, 2.0 us)
Async XLA Ops:
  0.6 0.9 %copy-start = (bf16[32,224]{1,0:T(8,128)(2,1)S(1)}, bf16[32,224]{1,0:T(8,128)(2,1)}, u32[]{:S(2)}) copy-start(bf16[32,224]{1,0:T(8,128)(2,1)} %param.9) | copy-start | bytes 43012
  0.6 16.9 %copy-start.1 = (bf16[2,8192]{1,0:T(2,128)(2,1)S(1)}, bf16[2,8192]{1,0:T(2,128)(2,1)}, u32[]{:S(2)}) copy-start(bf16[2,8192]{1,0:T(2,128)(2,1)} %param.10) | copy-start | bytes 98308
  0.7 19.8 %copy-start.2 = (bf16[8192]{0:T(1024)(128)(2,1)S(1)}, bf16[8192]{0:T(1024)(128)(2,1)}, u32[]{:S(2)}) copy-start(bf16[8192]{0:T(1024)(128)(2,1)} %param.12) | copy-start | bytes 49156
  0.7 30.0 %copy-start.3 = (s32[2]{0:T(128)S(1)}, s32[2]{0:T(128)}, u32[]{:S(2)}) copy-start(s32[2]{0:T(128)} %param.15) | copy-start | bytes 28
  0.7 34.7 %copy-start.5 = (s32[32]{0:T(128)S(1)}, s32[32]{0:T(128)}, u32[]{:S(2)}) copy-start(s32[32]{0:T(128)} %param.14) | copy-start | bytes 388
  4.5 51.3 %copy-start.4 = (f32[2]{0:T(128)S(1)}, f32[2]{0:T(128)}, u32[]{:S(2)}) copy-start(f32[2]{0:T(128)} %param.16) | copy-start | bytes 28
  4.6 2.1 %collective-permute-start = (f32[16,8192]{1,0:T(8,128)S(1)}, f32[16,8192]{1,0:T(8,128)S(1)}, u32[]{:S(2)}, u32[]{:S(2)}) collective-permute-start(f32[16,8192]{1,0:T(8,128)S(1)} %slice.119), channel_id=1, source_target_pairs={{0,1},{1,0},{2,3},{3,2},{4,5},{5,4},{6,7},{7,6},{8,9},{9,8},{10,11... | collective-permute-start | bytes 1572872 | tf_op jit(solution)/shard_map/ppermute | solution.py:30
  6.8 8.2 %collective-permute-start.1 = (f32[4,8192]{1,0:T(4,128)S(1)}, f32[4,8192]{1,0:T(4,128)S(1)}, u32[]{:S(2)}, u32[]{:S(2)}) collective-permute-start(f32[4,8192]{1,0:T(4,128)S(1)} %get-tuple-element.6), channel_id=1, source_target_pairs={{0,6},{1,7},{2,4},{3,5},{4,2},{5,3},{6,0},{7,1},{8,14},{9,15},{10,... | collective-permute-start | bytes 393224 | tf_op jit(solution)/shard_map/ppermute | solution.py:30
  10.7 6.8 %collective-permute-start.2 = (f32[4,8192]{1,0:T(4,128)S(1)}, f32[4,8192]{1,0:T(4,128)S(1)}, u32[]{:S(2)}, u32[]{:S(2)}) collective-permute-start(f32[4,8192]{1,0:T(4,128)S(1)} %get-tuple-element.8), channel_id=1, source_target_pairs={{0,4},{1,5},{2,6},{3,7},{4,0},{5,1},{6,2},{7,3},{8,12},{9,13},{10,... | collective-permute-start | bytes 393224 | tf_op jit(solution)/shard_map/ppermute | solution.py:30
  11.2 6.3 %collective-permute-start.3 = (f32[4,8192]{1,0:T(4,128)S(1)}, f32[4,8192]{1,0:T(4,128)S(1)}, u32[]{:S(2)}, u32[]{:S(2)}) collective-permute-start(f32[4,8192]{1,0:T(4,128)S(1)} %get-tuple-element.7), channel_id=1, source_target_pairs={{0,2},{1,3},{2,0},{3,1},{4,6},{5,7},{6,4},{7,5},{8,10},{9,11},{10,... | collective-permute-start | bytes 393224 | tf_op jit(solution)/shard_map/ppermute | solution.py:30
  17.8 8.7 %collective-permute-start.4 = (f32[2,2,8192]{2,1,0:T(2,128)S(1)}, f32[2,2,8192]{2,1,0:T(2,128)S(1)}, u32[]{:S(2)}, u32[]{:S(2)}) collective-permute-start(f32[2,2,8192]{2,1,0:T(2,128)S(1)} %reshape.120), channel_id=1, source_target_pairs={{0,8},{1,9},{2,10},{3,11},{4,12},{5,13},{6,14},{7,15},{8,0},{9,1},... | collective-permute-start | bytes 393224 | tf_op jit(solution)/shard_map/ppermute | solution.py:30
  27.1 4.9 %collective-permute-start.5 = (bf16[4,8192]{1,0:T(4,128)(2,1)S(1)}, bf16[4,8192]{1,0:T(4,128)(2,1)S(1)}, u32[]{:S(2)}, u32[]{:S(2)}) collective-permute-start(bf16[4,8192]{1,0:T(4,128)(2,1)S(1)} %multiply_convert_fusion), channel_id=1, source_target_pairs={{0,2},{1,3},{2,0},{3,1},{4,6},{5,7},{6,4},{7,5},{8,10},{9,11},{10,... | collective-permute-start | bytes 196616 | tf_op jit(solution)/shard_map/ppermute | solution.py:30
  29.1 4.3 %collective-permute-start.6 = (bf16[4,8192]{1,0:T(4,128)(2,1)S(1)}, bf16[4,8192]{1,0:T(4,128)(2,1)S(1)}, u32[]{:S(2)}, u32[]{:S(2)}) collective-permute-start(bf16[4,8192]{1,0:T(4,128)(2,1)S(1)} %multiply_convert_fusion), channel_id=1, source_target_pairs={{0,4},{1,5},{2,6},{3,7},{4,0},{5,1},{6,2},{7,3},{8,12},{9,13},{10,... | collective-permute-start | bytes 196616 | tf_op jit(solution)/shard_map/ppermute | solution.py:30
  29.8 5.2 %collective-permute-start.7 = (bf16[4,8192]{1,0:T(4,128)(2,1)S(1)}, bf16[4,8192]{1,0:T(4,128)(2,1)S(1)}, u32[]{:S(2)}, u32[]{:S(2)}) collective-permute-start(bf16[4,8192]{1,0:T(4,128)(2,1)S(1)} %multiply_convert_fusion), channel_id=1, source_target_pairs={{0,6},{1,7},{2,4},{3,5},{4,2},{5,3},{6,0},{7,1},{8,14},{9,15},{10,... | collective-permute-start | bytes 196616 | tf_op jit(solution)/shard_map/ppermute | solution.py:30
  35.1 1.6 %collective-permute-start.8 = (bf16[16,8192]{1,0:T(8,128)(2,1)S(1)}, bf16[16,8192]{1,0:T(8,128)(2,1)S(1)}, u32[]{:S(2)}, u32[]{:S(2)}) collective-permute-start(bf16[16,8192]{1,0:T(8,128)(2,1)S(1)} %pad_maximum_fusion), channel_id=1, source_target_pairs={{0,1},{1,0},{2,3},{3,2},{4,5},{5,4},{6,7},{7,6},{8,9},{9,8},{10,11... | collective-permute-start | bytes 786440 | tf_op jit(solution)/shard_map/ppermute | solution.py:30
  43.2 1.2 %collective-permute-start.9 = (f32[16,3]{0,1:T(4,128)S(1)}, f32[16,3]{0,1:T(4,128)S(1)}, u32[]{:S(2)}, u32[]{:S(2)}) collective-permute-start(f32[16,3]{0,1:T(4,128)S(1)} %slice.108), channel_id=1, source_target_pairs={{0,1},{1,0},{2,3},{3,2},{4,5},{5,4},{6,7},{7,6},{8,9},{9,8},{10,11... | collective-permute-start | bytes 584 | tf_op jit(solution)/shard_map/ppermute | solution.py:30
  44.4 4.5 %collective-permute-start.10 = (f32[4,3]{0,1:T(4,128)S(1)}, f32[4,3]{0,1:T(4,128)S(1)}, u32[]{:S(2)}, u32[]{:S(2)}) collective-permute-start(f32[4,3]{0,1:T(4,128)S(1)} %get-tuple-element.13), channel_id=1, source_target_pairs={{0,6},{1,7},{2,4},{3,5},{4,2},{5,3},{6,0},{7,1},{8,14},{9,15},{10,... | collective-permute-start | bytes 152 | tf_op jit(solution)/shard_map/ppermute | solution.py:30
  45.3 3.6 %collective-permute-start.11 = (f32[4,3]{0,1:T(4,128)S(1)}, f32[4,3]{0,1:T(4,128)S(1)}, u32[]{:S(2)}, u32[]{:S(2)}) collective-permute-start(f32[4,3]{0,1:T(4,128)S(1)} %get-tuple-element.15), channel_id=1, source_target_pairs={{0,4},{1,5},{2,6},{3,7},{4,0},{5,1},{6,2},{7,3},{8,12},{9,13},{10,... | collective-permute-start | bytes 152 | tf_op jit(solution)/shard_map/ppermute | solution.py:30
  46.5 3.6 %collective-permute-start.12 = (f32[4,3]{0,1:T(4,128)S(1)}, f32[4,3]{0,1:T(4,128)S(1)}, u32[]{:S(2)}, u32[]{:S(2)}) collective-permute-start(f32[4,3]{0,1:T(4,128)S(1)} %get-tuple-element.14), channel_id=1, source_target_pairs={{0,2},{1,3},{2,0},{3,1},{4,6},{5,7},{6,4},{7,5},{8,10},{9,11},{10,... | collective-permute-start | bytes 152 | tf_op jit(solution)/shard_map/ppermute | solution.py:30
  50.1 4.5 %collective-permute-start.13 = (f32[2,3]{0,1:T(4,128)S(1)}, f32[2,3]{0,1:T(4,128)S(1)}, u32[]{:S(2)}, u32[]{:S(2)}) collective-permute-start(f32[2,3]{0,1:T(4,128)S(1)} %slice.114), channel_id=1, source_target_pairs={{0,8},{1,9},{2,10},{3,11},{4,12},{5,13},{6,14},{7,15},{8,0},{9,1},... | collective-permute-start | bytes 80 | tf_op jit(solution)/shard_map/ppermute | solution.py:30

commit v2 on v0

v2 whole, which is shorter than its diff:
```python
import functools

import jax
import jax.numpy as jnp
from jax import lax
from jax.experimental import pallas as pl
from jax.experimental.pallas import tpu as pltpu
from jax.sharding import PartitionSpec as P

AXIS = "stream"
F32 = jnp.float32
BF16 = jnp.bfloat16
I32 = jnp.int32
WHOLE = pl.BlockSpec(memory_space=pltpu.VMEM)


def levels_of(devices):
    levels, stride = [(1, 2)], 2
    while stride < devices:
        size = 4 if (devices // stride) % 4 == 0 else 2
        levels.append((stride, size))
        stride *= size
    assert stride == devices
    return levels


def log2(number):
    assert number & (number - 1) == 0
    return number.bit_length() - 1


def swapped(block, distance):
    return lax.ppermute(block, AXIS, [(i, i ^ distance) for i in range(lax.axis_size(AXIS))])


def bytes_of(*arrays):
    return sum(a.size * a.dtype.itemsize for a in arrays)


def call(body, outs, *operands, extra=0, scratch=(), specs=None):
    shapes = [jax.ShapeDtypeStruct(shape, kind) for shape, kind in outs]
    return pl.pallas_call(
        body,
        out_shape=shapes,
        in_specs=specs or [WHOLE] * len(operands),
        out_specs=[WHOLE] * len(shapes),
        scratch_shapes=scratch,
        compiler_params=pltpu.CompilerParams(
            vmem_limit_bytes=bytes_of(*operands, *shapes) * 5 // 4 + extra + (2 << 20)
        ),
    )(*operands)


def token_at(place, levels, own):
    holder, inner = place >> log2(own), 1
    offset = jnp.zeros_like(place)
    for stride, size in reversed(levels):
        offset += ((holder >> log2(inner)) & (size - 1)) * stride
        inner *= size
    return (lax.axis_index(AXIS) ^ offset) * own + (place & (own - 1))


def ffn_kernel(levels, own, vocab_rows, *refs):
    sources, (keep_ref, send_ref, facts_ref, residual_ref, gain_ref, segments_ref, train_ref) = refs[:7], refs[7:14]
    hidden_ref, targets_ref, weights, arrived, loaded = refs[14:]
    hidden_hbm, targets_hbm, down_hbm = sources[:3]
    tokens = hidden_ref.shape[0]
    columns = down_hbm.shape[1] // CHUNKS
    copies = [
        pltpu.make_async_copy(
            down_hbm.at[:, pl.ds(c * columns, columns)], weights.at[c], arrived.at[c]
        )
        for c in range(CHUNKS)
    ]
    pairs = ((hidden_hbm, hidden_ref), (targets_hbm, targets_ref)) + tuple(
        zip(sources[3:], (residual_ref, gain_ref, segments_ref, train_ref))
    )
    small = [pltpu.make_async_copy(*pair, loaded.at[i]) for i, pair in enumerate(pairs)]
    small[0].start()
    for copy in copies + small[1:]:
        copy.start()
    square = (tokens, tokens)
    at_row = token_at(lax.broadcasted_iota(I32, square, 0), levels, own)
    chosen = at_row == lax.broadcasted_iota(I32, square, 1)
    small[0].wait()
    rows = jnp.dot(
        chosen.astype(F32).astype(BF16), hidden_ref[...], preferred_element_type=F32
    ).astype(BF16)
    for c in range(CHUNKS):
        copies[c].wait()
        part = jnp.dot(rows, weights[c], preferred_element_type=F32)
        keep_ref[:, c * columns : (c + 1) * columns] = part[: tokens // 2]
        send_ref[:, c * columns : (c + 1) * columns] = part[tokens // 2 :]
    for copy in small[1:]:
        copy.wait()
    wanted = jnp.sum(jnp.where(chosen, targets_ref[...], 0), axis=1, keepdims=True)
    diagonal = lax.broadcasted_iota(I32, square, 0) == lax.broadcasted_iota(I32, square, 1)
    wanted = jnp.sum(jnp.where(diagonal, wanted, 0), axis=0, keepdims=True)
    me = lax.axis_index(AXIS)
    facts_ref[0:1, :] = wanted - me * vocab_rows
    at_lane = token_at(lax.broadcasted_iota(I32, (1, tokens), 1), levels, own)
    following = jnp.zeros((1, tokens), I32)
    for j in range(own):
        following = jnp.where(at_lane + 1 == me * own + j, segments_ref[0:1, j : j + 1], following)
    facts_ref[1:2, :] = following


CHUNKS = 4


def add_kernel(came_count, keep_ref, *refs):
    total = keep_ref[...]
    for ref in refs[:came_count]:
        total += ref[...]
    outs = refs[came_count:]
    rows = total.shape[0] // len(outs)
    for k, out in enumerate(outs):
        out[...] = total[k * rows : (k + 1) * rows]


def add_residual_kernel(came_count, keep_ref, residual_ref, *refs):
    total = keep_ref[...]
    for ref in refs[:came_count]:
        total += ref[...]
    out = refs[came_count]
    own = residual_ref.shape[0]
    out[:own, :] = total[:own] + residual_ref[...].astype(F32)
    out[own:, :] = total[own:]


def norm_kernel(size, own, head_ref, gain_ref, mine_ref, *refs):
    del head_ref
    came, (states_ref, normed_ref) = refs[: size - 1], refs[size - 1 :]
    for place in range(size):
        total = mine_ref[place * own : (place + 1) * own, :]
        for k in range(1, size):
            total = total + came[k - 1][(place ^ k) * own : ((place ^ k) + 1) * own, :]
        states = total.astype(BF16)
        if place == 0:
            states_ref[...] = states
        values = states.astype(F32)
        scale = lax.rsqrt(jnp.mean(values * values, axis=1, keepdims=True) + 1e-05)
        for c in range(gain_ref.shape[0]):
            at = slice(c * 128, (c + 1) * 128)
            normed = values[:, at] * scale * gain_ref[c : c + 1, :].astype(F32)
            normed_ref[place * own : (place + 1) * own, at] = normed.astype(BF16)


def copy_kernel(source, out):
    out[...] = source[...]


def load_kernel(source, out, arrived):
    copy = pltpu.make_async_copy(source, out, arrived)
    copy.start()
    copy.wait()


def join_kernel(*refs):
    blocks, out = refs[1:-1], refs[-1]
    out[...] = jnp.concatenate([b[...].astype(F32) for b in blocks], axis=0).astype(BF16)


def loss_kernel(facts_ref, head_ref, near_ref, far_ref, keep_ref, send_ref):
    rows = jnp.concatenate([near_ref[...], far_ref[...]], axis=0)
    logits = lax.dot_general(
        head_ref[...], rows, (((1,), (1,)), ((), ())), preferred_element_type=F32
    )
    ids = lax.broadcasted_iota(I32, logits.shape, 0)
    half = rows.shape[0] // 2
    total = jnp.sum(jnp.exp(logits), axis=0, keepdims=True)
    picked = jnp.sum(jnp.where(ids == facts_ref[0:1, :], logits, 0.0), axis=0, keepdims=True)
    for row, values in enumerate((total, picked, facts_ref[1:2, :].astype(F32))):
        keep_ref[row : row + 1, :] = values[:, :half]
        send_ref[row : row + 1, :] = values[:, half:]


def add_lanes_kernel(came_count, keep_ref, *refs):
    total = keep_ref[...]
    for ref in refs[:came_count]:
        total += ref[...]
    outs = refs[came_count:]
    lanes = total.shape[1] // len(outs)
    for k, out in enumerate(outs):
        out[...] = total[:, k * lanes : (k + 1) * lanes]


def weight_kernel(tokens, came_count, segments_ref, train_ref, keep_ref, *refs):
    total = keep_ref[...]
    for ref in refs[:came_count]:
        total += ref[...]
    out = refs[came_count]
    own = out.shape[1]
    ref_loss = jnp.log(total[0:1]) - total[1:2]
    places = lax.axis_index(AXIS) * own + lax.broadcasted_iota(I32, (1, own), 1)
    same = (places + 1 < tokens) & (total[2:3].astype(I32) == segments_ref[...])
    out[...] = jnp.where(same, jax.nn.sigmoid(train_ref[...] - ref_loss), 0.0)


def on_device(
    hidden_units, residual, down_weight, final_gain, head_weight, targets, segments, train_loss
):
    own, width = residual.shape
    tokens, depth = hidden_units.shape
    levels = levels_of(lax.axis_size(AXIS))
    segments, train_loss = segments[None, :], train_loss[None, :]

    half = (tokens // 2, width)
    gain = final_gain.reshape(-1, 128)
    sources = [hidden_units, targets[None, :], down_weight, residual, gain, segments, train_loss]
    keep, send, facts, residual, gain, segments, train_loss = call(
        functools.partial(ffn_kernel, levels, own, head_weight.shape[0]),
        [(half, F32), (half, F32), ((2, tokens), I32)] + [(a.shape, a.dtype) for a in sources[3:]],
        *[pltpu.with_memory_space_constraint(a, pltpu.HBM) for a in sources],
        extra=bytes_of(down_weight),
        scratch=(
            pltpu.VMEM(hidden_units.shape, BF16),
            pltpu.VMEM((1, tokens), I32),
            pltpu.VMEM((CHUNKS, depth, width // CHUNKS), BF16),
            pltpu.SemaphoreType.DMA((CHUNKS,)),
            pltpu.SemaphoreType.DMA((6,)),
        ),
        specs=[pl.BlockSpec(memory_space=pltpu.HBM)] * 7,
    )
    came, rows = [swapped(send, 1)], tokens // 2
    for stride, size in levels[1:-1]:
        rows //= size
        keep, *parts = call(
            functools.partial(add_kernel, len(came)), [((rows, width), F32)] * size, keep, *came
        )
        came = [swapped(parts[k - 1], stride * k) for k in range(1, size)]
    stride, size = levels[-1]
    (mine,) = call(
        functools.partial(add_residual_kernel, len(came)), [((rows, width), F32)], keep, residual, *came
    )
    came = [swapped(mine, stride * k) for k in range(1, size)]
    (head,) = call(
        load_kernel,
        [(head_weight.shape, BF16)],
        pltpu.with_memory_space_constraint(head_weight, pltpu.HBM),
        scratch=(pltpu.SemaphoreType.DMA,),
        specs=[pl.BlockSpec(memory_space=pltpu.HBM)],
    )
    states, block = call(
        functools.partial(norm_kernel, size, own),
        [((own, width), BF16), ((rows, width), BF16)],
        head,
        gain,
        mine,
        *came,
        specs=[pl.BlockSpec(memory_space=pl.ANY)] + [WHOLE] * (size + 1),
    )
    (hidden_states,) = call(copy_kernel, [(states.shape, BF16)], states)
    for stride, size in levels[-2:0:-1]:
        came = [swapped(block, stride * k) for k in range(1, size)]
        (block,) = call(
            join_kernel,
            [((rows * size, width), BF16)],
            pltpu.with_memory_space_constraint(hidden_states, pltpu.HBM),
            block,
            *came,
            extra=bytes_of(block) * 8,
            specs=[pl.BlockSpec(memory_space=pltpu.HBM)] + [WHOLE] * size,
        )
        rows *= size
    far = swapped(block, 1)

    keep, send = call(
        loss_kernel,
        [((3, tokens // 2), F32)] * 2,
        facts,
        head,
        block,
        far,
        extra=2 * bytes_of(block),
    )
    came, lanes = [swapped(send, 1)], tokens // 2
    for stride, size in levels[1:]:
        lanes //= size
        keep, *parts = call(
            functools.partial(add_lanes_kernel, len(came)), [((3, lanes), F32)] * size, keep, *came
        )
        came = [swapped(parts[k - 1], stride * k) for k in range(1, size)]
    (loss_weight,) = call(
        functools.partial(weight_kernel, tokens, len(came)), [((1, own), F32)], segments, train_loss, keep, *came
    )
    return (hidden_states, loss_weight.reshape(own))


def solution(mesh):
    placed = (
        P("groups", "stream"),
        P(("groups", "stream"), None),
        P("stream", None),
        P(),
        P("stream", None),
        P("groups"),
        P(("groups", "stream")),
        P(("groups", "stream")),
    )
    return jax.shard_map(
        on_device,
        mesh=mesh,
        in_specs=placed,
        out_specs=(P(("groups", "stream"), None), P(("groups", "stream"))),
        check_vma=False,
    )
```

time: 157 us -> 48.9 us (0.31)
  blocking collectives: 56.8 us -> 0 us
  waiting for transfers between devices: 65.4 us -> 19.5 us
  starting transfers between devices: 1.32 us -> 18.5 us
  between operations: 14.7 us -> 0.69 us
  Pallas kernels: 0 us -> 10.1 us
  matrix products: 9.95 us -> 0 us
  local copies, waits for them, and re-layouts: 4.05 us -> 0 us
  other arithmetic: 4.02 us -> 0 us
    psum x1 -> x0, waiting for transfers between devices: 65.4 us -> none  [on_device(): lax.psum(jnp.dot(hidden_units, down_weight, preferred_element_type=jnp.fl...]
    unnamed x1 -> x0, blocking collectives: 30.6 us -> none
    all_gather x1 -> x0, blocking collectives: 26.2 us -> none  [on_device(): all_rows = lax.all_gather(residual, 'stream', axis=0, tiled=True)]
    ppermute x1 -> x14, waiting for transfers between devices: 0.01 us -> 19.5 us  [swapped(): lax.ppermute(block, AXIS, [(i, i ^ distance) for i in range(lax.axis_size...]
    ppermute x1 -> x14, starting transfers between devices: 1.28 us -> 18.5 us  [swapped(): lax.ppermute(block, AXIS, [(i, i ^ distance) for i in range(lax.axis_size...]
    pallas_call x0 -> x11, Pallas kernels: none -> 10.1 us  [call(): pl.pallas_call(body, out_shape=shapes, in_specs=specs or [WHOLE] * len(op...]
    dot_general x2 -> x0, matrix products: 9.95 us -> none  [the longest x1 6.11 us: vocab_terms(): jnp.einsum('td,vd->tv', rows, head_weight, preferred_element_type=jnp.flo...]
    unnamed x9 -> x0, local copies, waits for them, and re-layouts: 1.91 us -> none
  transfers between devices with their start and end apart: 2 -> 14, of which waited for: 1 -> 14; matrix products, arithmetic and copies ran while one was open for 7% -> 0% of each run, Pallas kernels for 0% -> 8%
where the time goes in v2:
time: 48.9 us; the launch traced here: 48.7 us
  waiting for transfers between devices  19.5 us (40%)
  starting transfers between devices  18.5 us (38%)
  Pallas kernels  10.1 us (21%)
  between operations  0.69 us (1%)
    ppermute x14, waiting for transfers between devices, swapped(): lax.ppermute(block, AXIS, [(i, i ^ distance) for i in range(lax.axis_size...  19.5 us
    ppermute x14, starting transfers between devices, swapped(): lax.ppermute(block, AXIS, [(i, i ^ distance) for i in range(lax.axis_size...  18.5 us
    pallas_call x11, Pallas kernels, call(): pl.pallas_call(body, out_shape=shapes, in_specs=specs or [WHOLE] * len(op...  10.1 us
  transfers between devices with their start and end apart: 14, of which 14 were waited for; matrix products, arithmetic and copies ran while one was open for 0% of the time, Pallas kernels for 8%

profile of v2, /device:TPU:0, one launch (start us, length us, event | category | flops | bytes accessed | tf_op | source)
XLA Modules:
  0.0 48.7 jit_solution(15206910211955618502)
XLA Ops:
  0.6 2.6 %shard_map.96 = (f32[16,8192]{1,0:T(8,128)S(1)}, f32[16,8192]{1,0:T(8,128)S(1)}, s32[2,32]{1,0:T(2,128)S(1)}, bf16[2,8192]{1,0:T(2,128)(2,1)S(1)}, bf16[64,128]{...) custom-call(bf16[32,224]{1,0:T(8,128)(2,1)} %refs_0_.1, s32[1,32]{1,0:T(1,128)} %bitcast.6, ...), custom_call_target="tpu_custom_call" | custom-call | tf_op jit(solution)/shard_map/pallas_call | solution.py:42
  3.2 0.5 %collective-permute-start = (f32[16,8192]{1,0:T(8,128)S(1)}, f32[16,8192]{1,0:T(8,128)S(1)}, u32[]{:S(2)}, u32[]{:S(2)}) collective-permute-start(f32[16,8192]{1,0:T(8,128)S(1)} %get-tuple-element.25), channel_id=1, source_target_pairs={{0,1},{1,0},{2,3},{3,2},{4,5},{5,4},{6,7},{7,6},{8,9},{9,8},{10,11... | collective-permute-start | bytes 1572872 | tf_op jit(solution)/shard_map/ppermute | solution.py:33
  3.7 1.5 %collective-permute-done.refs_0_ = f32[16,8192]{1,0:T(8,128)S(1)} collective-permute-done((f32[16,8192]{1,0:T(8,128)S(1)}, f32[16,8192]{1,0:T(8,128)S(1)}, u32[]{:S(2)}, u32[]{:S(2)}) %collective-permute-start) | collective-permute-done | bytes 524320 | tf_op jit(solution)/shard_map/ppermute | solution.py:33
  5.4 3.0 %collective-permute-start.1 = (f32[4,8192]{1,0:T(4,128)S(1)}, f32[4,8192]{1,0:T(4,128)S(1)}, u32[]{:S(2)}, u32[]{:S(2)}) collective-permute-start(f32[4,8192]{1,0:T(4,128)S(1)} %get-tuple-element.28), channel_id=1, source_target_pairs={{0,2},{1,3},{2,0},{3,1},{4,6},{5,7},{6,4},{7,5},{8,10},{9,11},{10,... | collective-permute-start | bytes 393224 | tf_op jit(solution)/shard_map/ppermute | solution.py:33
  8.3 1.6 %collective-permute-start.2 = (f32[4,8192]{1,0:T(4,128)S(1)}, f32[4,8192]{1,0:T(4,128)S(1)}, u32[]{:S(2)}, u32[]{:S(2)}) collective-permute-start(f32[4,8192]{1,0:T(4,128)S(1)} %get-tuple-element.29), channel_id=1, source_target_pairs={{0,4},{1,5},{2,6},{3,7},{4,0},{5,1},{6,2},{7,3},{8,12},{9,13},{10,... | collective-permute-start | bytes 393224 | tf_op jit(solution)/shard_map/ppermute | solution.py:33
  9.9 2.2 %collective-permute-done.1.refs_0_ = f32[4,8192]{1,0:T(4,128)S(1)} collective-permute-done((f32[4,8192]{1,0:T(4,128)S(1)}, f32[4,8192]{1,0:T(4,128)S(1)}, u32[]{:S(2)}, u32[]{:S(2)}) %collective-permute-start.1) | collective-permute-done | bytes 131104 | tf_op jit(solution)/shard_map/ppermute | solution.py:33
  12.1 2.6 %collective-permute-done.2.refs_1_ = f32[4,8192]{1,0:T(4,128)S(1)} collective-permute-done((f32[4,8192]{1,0:T(4,128)S(1)}, f32[4,8192]{1,0:T(4,128)S(1)}, u32[]{:S(2)}, u32[]{:S(2)}) %collective-permute-start.2) | collective-permute-done | bytes 131104 | tf_op jit(solution)/shard_map/ppermute | solution.py:33
  14.7 1.5 %collective-permute-done.3.refs_2_ = f32[4,8192]{1,0:T(4,128)S(1)} collective-permute-done((f32[4,8192]{1,0:T(4,128)S(1)}, f32[4,8192]{1,0:T(4,128)S(1)}, u32[]{:S(2)}, u32[]{:S(2)}) %collective-permute-start.3) | collective-permute-done | bytes 131104 | tf_op jit(solution)/shard_map/ppermute | solution.py:33
  16.2 2.8 %collective-permute-start.4 = (f32[4,8192]{1,0:T(4,128)S(1)}, f32[4,8192]{1,0:T(4,128)S(1)}, u32[]{:S(2)}, u32[]{:S(2)}) collective-permute-start(f32[4,8192]{1,0:T(4,128)S(1)} %shard_map.98.mine_ref), channel_id=1, source_target_pairs={{0,8},{1,9},{2,10},{3,11},{4,12},{5,13},{6,14},{7,15},{8,0},{9,1},... | collective-permute-start | bytes 393224 | tf_op jit(solution)/shard_map/ppermute | solution.py:33
  19.0 3.4 %shard_map.95.head_ref = bf16[512,8192]{1,0:T(8,128)(2,1)S(1)} custom-call(bf16[512,8192]{1,0:T(8,128)(2,1)} %source.1), custom_call_target="tpu_custom_call" | custom-call | tf_op jit(solution)/shard_map/pallas_call | solution.py:42
  22.4 2.3 %collective-permute-done.4.refs_0_ = f32[4,8192]{1,0:T(4,128)S(1)} collective-permute-done((f32[4,8192]{1,0:T(4,128)S(1)}, f32[4,8192]{1,0:T(4,128)S(1)}, u32[]{:S(2)}, u32[]{:S(2)}) %collective-permute-start.4) | collective-permute-done | bytes 131104 | tf_op jit(solution)/shard_map/ppermute | solution.py:33
  24.7 0.2 shard_map.99
  25.0 1.5 %collective-permute-start.7 = (bf16[4,8192]{1,0:T(4,128)(2,1)S(1)}, bf16[4,8192]{1,0:T(4,128)(2,1)S(1)}, u32[]{:S(2)}, u32[]{:S(2)}) collective-permute-start(bf16[4,8192]{1,0:T(4,128)(2,1)S(1)} %get-tuple-element.35.refs_1_), channel_id=1, source_target_pairs={{0,6},{1,7},{2,4},{3,5},{4,2},{5,3},{6,0},{7,1},{8,14},{9,15},{10,... | collective-permute-start | bytes 196616 | tf_op jit(solution)/shard_map/ppermute | solution.py:33
  26.5 1.4 %collective-permute-start.6 = (bf16[4,8192]{1,0:T(4,128)(2,1)S(1)}, bf16[4,8192]{1,0:T(4,128)(2,1)S(1)}, u32[]{:S(2)}, u32[]{:S(2)}) collective-permute-start(bf16[4,8192]{1,0:T(4,128)(2,1)S(1)} %get-tuple-element.35.refs_1_), channel_id=1, source_target_pairs={{0,4},{1,5},{2,6},{3,7},{4,0},{5,1},{6,2},{7,3},{8,12},{9,13},{10,... | collective-permute-start | bytes 196616 | tf_op jit(solution)/shard_map/ppermute | solution.py:33
  27.8 0.7 %collective-permute-start.5 = (bf16[4,8192]{1,0:T(4,128)(2,1)S(1)}, bf16[4,8192]{1,0:T(4,128)(2,1)S(1)}, u32[]{:S(2)}, u32[]{:S(2)}) collective-permute-start(bf16[4,8192]{1,0:T(4,128)(2,1)S(1)} %get-tuple-element.35.refs_1_), channel_id=1, source_target_pairs={{0,2},{1,3},{2,0},{3,1},{4,6},{5,7},{6,4},{7,5},{8,10},{9,11},{10,... | collective-permute-start | bytes 196616 | tf_op jit(solution)/shard_map/ppermute | solution.py:33
  28.5 0.6 %shard_map.100.refs_0_ = bf16[2,8192]{1,0:T(2,128)(2,1)} custom-call(bf16[2,8192]{1,0:T(2,128)(2,1)S(1)} %get-tuple-element.31.source), custom_call_target="tpu_custom_call" | custom-call | tf_op jit(solution)/shard_map/pallas_call | solution.py:42
  29.1 1.1 %collective-permute-done.7.refs_4_ = bf16[4,8192]{1,0:T(4,128)(2,1)S(1)} collective-permute-done((bf16[4,8192]{1,0:T(4,128)(2,1)S(1)}, bf16[4,8192]{1,0:T(4,128)(2,1)S(1)}, u32[]{:S(2)}, u32[]{:S(2)}) %collective-permute-start.7) | collective-permute-done | bytes 65568 | tf_op jit(solution)/shard_map/ppermute | solution.py:33
  30.2 0.6 %collective-permute-done.6.refs_3_ = bf16[4,8192]{1,0:T(4,128)(2,1)S(1)} collective-permute-done((bf16[4,8192]{1,0:T(4,128)(2,1)S(1)}, bf16[4,8192]{1,0:T(4,128)(2,1)S(1)}, u32[]{:S(2)}, u32[]{:S(2)}) %collective-permute-start.6) | collective-permute-done | bytes 65568 | tf_op jit(solution)/shard_map/ppermute | solution.py:33
  30.8 1.3 %collective-permute-done.5.refs_2_ = bf16[4,8192]{1,0:T(4,128)(2,1)S(1)} collective-permute-done((bf16[4,8192]{1,0:T(4,128)(2,1)S(1)}, bf16[4,8192]{1,0:T(4,128)(2,1)S(1)}, u32[]{:S(2)}, u32[]{:S(2)}) %collective-permute-start.5) | collective-permute-done | bytes 65568 | tf_op jit(solution)/shard_map/ppermute | solution.py:33
  32.2 1.5 %collective-permute-done.8.far_ref = bf16[16,8192]{1,0:T(8,128)(2,1)S(1)} collective-permute-done((bf16[16,8192]{1,0:T(8,128)(2,1)S(1)}, bf16[16,8192]{1,0:T(8,128)(2,1)S(1)}, u32[]{:S(2)}, u32[]{:S(2)}) %collective-permute-start.8) | collective-permute-done | bytes 262176 | tf_op jit(solution)/shard_map/ppermute | solution.py:33
  33.8 2.4 %shard_map.102 = (f32[3,16]{1,0:T(4,128)S(1)}, f32[3,16]{1,0:T(4,128)S(1)}) custom-call(s32[2,32]{1,0:T(2,128)S(1)} %get-tuple-element.34.facts_ref, bf16[512,8192]{1,0:T(8,128)(2,1)S(1)} %shard_map.95.head_ref, bf16[16,8192]{1,0:T(8,128)(2,1)S(1)} %shard_map.101.near_ref, bf16[16,8192]{1,0:T(8,128)(2,1)S(1)} %collective-permute-done.8.far_ref), custom_call_target="tpu_custom_call" | custom-call | tf_op jit(solution)/shard_map/pallas_call | solution.py:42
  36.1 0.1 collective-permute-start.9
  36.3 1.0 %collective-permute-done.9.refs_0_ = f32[3,16]{1,0:T(4,128)S(1)} collective-permute-done((f32[3,16]{1,0:T(4,128)S(1)}, f32[3,16]{1,0:T(4,128)S(1)}, u32[]{:S(2)}, u32[]{:S(2)}) %collective-permute-start.9) | collective-permute-done | bytes 224 | tf_op jit(solution)/shard_map/ppermute | solution.py:33
  37.4 0.7 %collective-permute-start.10 = (f32[3,4]{1,0:T(4,128)S(1)}, f32[3,4]{1,0:T(4,128)S(1)}, u32[]{:S(2)}, u32[]{:S(2)}) collective-permute-start(f32[3,4]{1,0:T(4,128)S(1)} %get-tuple-element.39), channel_id=1, source_target_pairs={{0,2},{1,3},{2,0},{3,1},{4,6},{5,7},{6,4},{7,5},{8,10},{9,11},{10,... | collective-permute-start | bytes 152 | tf_op jit(solution)/shard_map/ppermute | solution.py:33
  38.1 0.6 %collective-permute-start.11 = (f32[3,4]{1,0:T(4,128)S(1)}, f32[3,4]{1,0:T(4,128)S(1)}, u32[]{:S(2)}, u32[]{:S(2)}) collective-permute-start(f32[3,4]{1,0:T(4,128)S(1)} %get-tuple-element.40), channel_id=1, source_target_pairs={{0,4},{1,5},{2,6},{3,7},{4,0},{5,1},{6,2},{7,3},{8,12},{9,13},{10,... | collective-permute-start | bytes 152 | tf_op jit(solution)/shard_map/ppermute | solution.py:33
  38.7 2.2 %collective-permute-start.12 = (f32[3,4]{1,0:T(4,128)S(1)}, f32[3,4]{1,0:T(4,128)S(1)}, u32[]{:S(2)}, u32[]{:S(2)}) collective-permute-start(f32[3,4]{1,0:T(4,128)S(1)} %get-tuple-element.41), channel_id=1, source_target_pairs={{0,6},{1,7},{2,4},{3,5},{4,2},{5,3},{6,0},{7,1},{8,14},{9,15},{10,... | collective-permute-start | bytes 152 | tf_op jit(solution)/shard_map/ppermute | solution.py:33
  40.9 0.1 collective-permute-done.10.refs_0_
  41.0 0.7 %collective-permute-done.11.refs_1_ = f32[3,4]{1,0:T(4,128)S(1)} collective-permute-done((f32[3,4]{1,0:T(4,128)S(1)}, f32[3,4]{1,0:T(4,128)S(1)}, u32[]{:S(2)}, u32[]{:S(2)}) %collective-permute-start.11) | collective-permute-done | bytes 80 | tf_op jit(solution)/shard_map/ppermute | solution.py:33
  41.7 1.5 %collective-permute-done.12.refs_2_ = f32[3,4]{1,0:T(4,128)S(1)} collective-permute-done((f32[3,4]{1,0:T(4,128)S(1)}, f32[3,4]{1,0:T(4,128)S(1)}, u32[]{:S(2)}, u32[]{:S(2)}) %collective-permute-start.12) | collective-permute-done | bytes 80 | tf_op jit(solution)/shard_map/ppermute | solution.py:33
  43.2 3.4 %collective-permute-start.13 = (f32[3,2]{1,0:T(4,128)S(1)}, f32[3,2]{1,0:T(4,128)S(1)}, u32[]{:S(2)}, u32[]{:S(2)}) collective-permute-start(f32[3,2]{1,0:T(4,128)S(1)} %get-tuple-element.43), channel_id=1, source_target_pairs={{0,8},{1,9},{2,10},{3,11},{4,12},{5,13},{6,14},{7,15},{8,0},{9,1},... | collective-permute-start | bytes 80 | tf_op jit(solution)/shard_map/ppermute | solution.py:33
  46.6 1.6 %collective-permute-done.13.refs_0_ = f32[3,2]{1,0:T(4,128)S(1)} collective-permute-done((f32[3,2]{1,0:T(4,128)S(1)}, f32[3,2]{1,0:T(4,128)S(1)}, u32[]{:S(2)}, u32[]{:S(2)}) %collective-permute-start.13) | collective-permute-done | bytes 56 | tf_op jit(solution)/shard_map/ppermute | solution.py:33
  48.2 0.5 %shard_map.105 = f32[1,2]{1,0:T(1,128)} custom-call(s32[1,2]{1,0:T(1,128)S(1)} %get-tuple-element.32.segments_ref, f32[1,2]{1,0:T(1,128)S(1)} %get-tuple-element.33.train_ref, f32[3,2]{1,0:T(4,128)S(1)} %get-tuple-element.42.keep_ref, f32[3,2]{1,0:T(4,128)S(1)} %collective-permute-done.13.refs_0_), custom_call_target="tpu_custom_call" | custom-call | tf_op jit(solution)/shard_map/pallas_call | solution.py:42
  (7 shorter events, 0.4 us)
Async XLA Ops:
  3.2 2.1 %collective-permute-start = (f32[16,8192]{1,0:T(8,128)S(1)}, f32[16,8192]{1,0:T(8,128)S(1)}, u32[]{:S(2)}, u32[]{:S(2)}) collective-permute-start(f32[16,8192]{1,0:T(8,128)S(1)} %get-tuple-element.25), channel_id=1, source_target_pairs={{0,1},{1,0},{2,3},{3,2},{4,5},{5,4},{6,7},{7,6},{8,9},{9,8},{10,11... | collective-permute-start | bytes 1572872 | tf_op jit(solution)/shard_map/ppermute | solution.py:33
  5.4 6.7 %collective-permute-start.1 = (f32[4,8192]{1,0:T(4,128)S(1)}, f32[4,8192]{1,0:T(4,128)S(1)}, u32[]{:S(2)}, u32[]{:S(2)}) collective-permute-start(f32[4,8192]{1,0:T(4,128)S(1)} %get-tuple-element.28), channel_id=1, source_target_pairs={{0,2},{1,3},{2,0},{3,1},{4,6},{5,7},{6,4},{7,5},{8,10},{9,11},{10,... | collective-permute-start | bytes 393224 | tf_op jit(solution)/shard_map/ppermute | solution.py:33
  8.3 6.4 %collective-permute-start.2 = (f32[4,8192]{1,0:T(4,128)S(1)}, f32[4,8192]{1,0:T(4,128)S(1)}, u32[]{:S(2)}, u32[]{:S(2)}) collective-permute-start(f32[4,8192]{1,0:T(4,128)S(1)} %get-tuple-element.29), channel_id=1, source_target_pairs={{0,4},{1,5},{2,6},{3,7},{4,0},{5,1},{6,2},{7,3},{8,12},{9,13},{10,... | collective-permute-start | bytes 393224 | tf_op jit(solution)/shard_map/ppermute | solution.py:33
  9.9 6.3 %collective-permute-start.3 = (f32[4,8192]{1,0:T(4,128)S(1)}, f32[4,8192]{1,0:T(4,128)S(1)}, u32[]{:S(2)}, u32[]{:S(2)}) collective-permute-start(f32[4,8192]{1,0:T(4,128)S(1)} %get-tuple-element.30), channel_id=1, source_target_pairs={{0,6},{1,7},{2,4},{3,5},{4,2},{5,3},{6,0},{7,1},{8,14},{9,15},{10,... | collective-permute-start | bytes 393224 | tf_op jit(solution)/shard_map/ppermute | solution.py:33
  16.2 8.5 %collective-permute-start.4 = (f32[4,8192]{1,0:T(4,128)S(1)}, f32[4,8192]{1,0:T(4,128)S(1)}, u32[]{:S(2)}, u32[]{:S(2)}) collective-permute-start(f32[4,8192]{1,0:T(4,128)S(1)} %shard_map.98.mine_ref), channel_id=1, source_target_pairs={{0,8},{1,9},{2,10},{3,11},{4,12},{5,13},{6,14},{7,15},{8,0},{9,1},... | collective-permute-start | bytes 393224 | tf_op jit(solution)/shard_map/ppermute | solution.py:33
  25.0 5.2 %collective-permute-start.7 = (bf16[4,8192]{1,0:T(4,128)(2,1)S(1)}, bf16[4,8192]{1,0:T(4,128)(2,1)S(1)}, u32[]{:S(2)}, u32[]{:S(2)}) collective-permute-start(bf16[4,8192]{1,0:T(4,128)(2,1)S(1)} %get-tuple-element.35.refs_1_), channel_id=1, source_target_pairs={{0,6},{1,7},{2,4},{3,5},{4,2},{5,3},{6,0},{7,1},{8,14},{9,15},{10,... | collective-permute-start | bytes 196616 | tf_op jit(solution)/shard_map/ppermute | solution.py:33
  26.5 4.3 %collective-permute-start.6 = (bf16[4,8192]{1,0:T(4,128)(2,1)S(1)}, bf16[4,8192]{1,0:T(4,128)(2,1)S(1)}, u32[]{:S(2)}, u32[]{:S(2)}) collective-permute-start(bf16[4,8192]{1,0:T(4,128)(2,1)S(1)} %get-tuple-element.35.refs_1_), channel_id=1, source_target_pairs={{0,4},{1,5},{2,6},{3,7},{4,0},{5,1},{6,2},{7,3},{8,12},{9,13},{10,... | collective-permute-start | bytes 196616 | tf_op jit(solution)/shard_map/ppermute | solution.py:33
  27.8 4.3 %collective-permute-start.5 = (bf16[4,8192]{1,0:T(4,128)(2,1)S(1)}, bf16[4,8192]{1,0:T(4,128)(2,1)S(1)}, u32[]{:S(2)}, u32[]{:S(2)}) collective-permute-start(bf16[4,8192]{1,0:T(4,128)(2,1)S(1)} %get-tuple-element.35.refs_1_), channel_id=1, source_target_pairs={{0,2},{1,3},{2,0},{3,1},{4,6},{5,7},{6,4},{7,5},{8,10},{9,11},{10,... | collective-permute-start | bytes 196616 | tf_op jit(solution)/shard_map/ppermute | solution.py:33
  32.2 1.6 %collective-permute-start.8 = (bf16[16,8192]{1,0:T(8,128)(2,1)S(1)}, bf16[16,8192]{1,0:T(8,128)(2,1)S(1)}, u32[]{:S(2)}, u32[]{:S(2)}) collective-permute-start(bf16[16,8192]{1,0:T(8,128)(2,1)S(1)} %shard_map.101.near_ref), channel_id=1, source_target_pairs={{0,1},{1,0},{2,3},{3,2},{4,5},{5,4},{6,7},{7,6},{8,9},{9,8},{10,11... | collective-permute-start | bytes 786440 | tf_op jit(solution)/shard_map/ppermute | solution.py:33
  36.1 1.2 %collective-permute-start.9 = (f32[3,16]{1,0:T(4,128)S(1)}, f32[3,16]{1,0:T(4,128)S(1)}, u32[]{:S(2)}, u32[]{:S(2)}) collective-permute-start(f32[3,16]{1,0:T(4,128)S(1)} %get-tuple-element.37), channel_id=1, source_target_pairs={{0,1},{1,0},{2,3},{3,2},{4,5},{5,4},{6,7},{7,6},{8,9},{9,8},{10,11... | collective-permute-start | bytes 584 | tf_op jit(solution)/shard_map/ppermute | solution.py:33
  37.4 3.6 %collective-permute-start.10 = (f32[3,4]{1,0:T(4,128)S(1)}, f32[3,4]{1,0:T(4,128)S(1)}, u32[]{:S(2)}, u32[]{:S(2)}) collective-permute-start(f32[3,4]{1,0:T(4,128)S(1)} %get-tuple-element.39), channel_id=1, source_target_pairs={{0,2},{1,3},{2,0},{3,1},{4,6},{5,7},{6,4},{7,5},{8,10},{9,11},{10,... | collective-permute-start | bytes 152 | tf_op jit(solution)/shard_map/ppermute | solution.py:33
  38.1 3.6 %collective-permute-start.11 = (f32[3,4]{1,0:T(4,128)S(1)}, f32[3,4]{1,0:T(4,128)S(1)}, u32[]{:S(2)}, u32[]{:S(2)}) collective-permute-start(f32[3,4]{1,0:T(4,128)S(1)} %get-tuple-element.40), channel_id=1, source_target_pairs={{0,4},{1,5},{2,6},{3,7},{4,0},{5,1},{6,2},{7,3},{8,12},{9,13},{10,... | collective-permute-start | bytes 152 | tf_op jit(solution)/shard_map/ppermute | solution.py:33
  38.7 4.5 %collective-permute-start.12 = (f32[3,4]{1,0:T(4,128)S(1)}, f32[3,4]{1,0:T(4,128)S(1)}, u32[]{:S(2)}, u32[]{:S(2)}) collective-permute-start(f32[3,4]{1,0:T(4,128)S(1)} %get-tuple-element.41), channel_id=1, source_target_pairs={{0,6},{1,7},{2,4},{3,5},{4,2},{5,3},{6,0},{7,1},{8,14},{9,15},{10,... | collective-permute-start | bytes 152 | tf_op jit(solution)/shard_map/ppermute | solution.py:33
  43.2 4.9 %collective-permute-start.13 = (f32[3,2]{1,0:T(4,128)S(1)}, f32[3,2]{1,0:T(4,128)S(1)}, u32[]{:S(2)}, u32[]{:S(2)}) collective-permute-start(f32[3,2]{1,0:T(4,128)S(1)} %get-tuple-element.43), channel_id=1, source_target_pairs={{0,8},{1,9},{2,10},{3,11},{4,12},{5,13},{6,14},{7,15},{8,0},{9,1},... | collective-permute-start | bytes 80 | tf_op jit(solution)/shard_map/ppermute | solution.py:33

commit v3 on v2

v3 whole, which is shorter than its diff:
```python
import functools

import jax
import jax.numpy as jnp
from jax import lax
from jax.experimental import pallas as pl
from jax.experimental.pallas import tpu as pltpu
from jax.sharding import PartitionSpec as P

AXIS = "stream"
F32 = jnp.float32
BF16 = jnp.bfloat16
F16 = jnp.float16
I32 = jnp.int32
WHOLE = pl.BlockSpec(memory_space=pltpu.VMEM)
IN_HBM = pl.BlockSpec(memory_space=pltpu.HBM)
ANYWHERE = pl.BlockSpec(memory_space=pl.ANY)
CHUNKS = 4


def levels_of(devices, crossed):
    levels, stride = [(0, 1)], 2
    while stride < devices:
        if (devices // stride) % 4 == 0:
            levels.append((0, stride | crossed, 2 * stride | crossed, 3 * stride))
        else:
            levels.append((0, stride | crossed))
        stride *= len(levels[-1])
    assert stride == devices
    return levels


def log2(number):
    assert number & (number - 1) == 0
    return number.bit_length() - 1


def swapped(block, distance):
    return lax.ppermute(block, AXIS, [(i, i ^ distance) for i in range(lax.axis_size(AXIS))])


def bytes_of(*arrays):
    return sum(a.size * a.dtype.itemsize for a in arrays)


def call(body, outs, *operands, extra=0, scratch=(), specs=None):
    shapes = [jax.ShapeDtypeStruct(shape, kind) for shape, kind in outs]
    return pl.pallas_call(
        body,
        out_shape=shapes,
        in_specs=specs or [WHOLE] * len(operands),
        out_specs=[WHOLE] * len(shapes),
        scratch_shapes=scratch,
        compiler_params=pltpu.CompilerParams(
            vmem_limit_bytes=bytes_of(*operands, *shapes) * 5 // 4 + extra + (2 << 20)
        ),
    )(*operands)


def distance_at(holder, levels):
    distance, inner = jnp.zeros_like(holder), 0
    for level in reversed(levels):
        digit = holder >> inner
        for bit in range(log2(len(level))):
            distance ^= ((digit >> bit) & 1) * level[1 << bit]
        inner += log2(len(level))
    return distance


def token_at(place, levels, own):
    distance = distance_at(place >> log2(own), levels)
    return (lax.axis_index(AXIS) ^ distance) * own + (place & (own - 1))


def ffn_kernel(levels, gather_levels, own, vocab_rows, *refs):
    sources, (keep_ref, send_ref, facts_ref, residual_ref, gain_ref, segments_ref, train_ref) = refs[:7], refs[7:14]
    hidden_ref, targets_ref, weights, arrived, loaded = refs[14:]
    hidden_hbm, targets_hbm, down_hbm = sources[:3]
    tokens = hidden_ref.shape[0]
    columns = down_hbm.shape[1] // CHUNKS
    copies = [
        pltpu.make_async_copy(
            down_hbm.at[:, pl.ds(c * columns, columns)], weights.at[c], arrived.at[c]
        )
        for c in range(CHUNKS)
    ]
    pairs = ((hidden_hbm, hidden_ref), (targets_hbm, targets_ref)) + tuple(
        zip(sources[3:], (residual_ref, gain_ref, segments_ref, train_ref))
    )
    small = [pltpu.make_async_copy(*pair, loaded.at[i]) for i, pair in enumerate(pairs)]
    small[0].start()
    for copy in copies + small[1:]:
        copy.start()
    square = (tokens, tokens)
    sublane, lane = (lax.broadcasted_iota(I32, square, d) for d in (0, 1))
    chosen = token_at(sublane, levels, own) == lane
    small[0].wait()
    rows = jnp.dot(
        chosen.astype(F32).astype(BF16), hidden_ref[...], preferred_element_type=F32
    ).astype(BF16)
    for c in range(CHUNKS):
        copies[c].wait()
        part = jnp.dot(rows, weights[c], preferred_element_type=F32)
        keep_ref[:, c * columns : (c + 1) * columns] = part[: tokens // 2]
        send_ref[:, c * columns : (c + 1) * columns] = part[tokens // 2 :]
    for copy in small[1:]:
        copy.wait()
    chosen = token_at(sublane, gather_levels, own) == lane
    wanted = jnp.sum(jnp.where(chosen, targets_ref[...], 0), axis=1, keepdims=True)
    wanted = jnp.sum(jnp.where(sublane == lane, wanted, 0), axis=0, keepdims=True)
    me = lax.axis_index(AXIS)
    facts_ref[0:1, :] = wanted - me * vocab_rows
    at_lane = token_at(lax.broadcasted_iota(I32, (1, tokens), 1), gather_levels, own)
    following = jnp.zeros((1, tokens), I32)
    for j in range(own):
        following = jnp.where(at_lane + 1 == me * own + j, segments_ref[0:1, j : j + 1], following)
    facts_ref[1:2, :] = following


def norm_kernel(own, total_ref, gain_ref, states_ref, normed_ref):
    states = total_ref[...].astype(BF16)
    states_ref[...] = states[:own]
    values = states.astype(F32)
    scale = lax.rsqrt(jnp.mean(values * values, axis=1, keepdims=True) + 1e-05)
    for c in range(gain_ref.shape[0]):
        at = slice(c * 128, (c + 1) * 128)
        normed_ref[:, at] = (values[:, at] * scale * gain_ref[c : c + 1, :].astype(F32)).astype(BF16)


def copy_kernel(source, out):
    out[...] = source[...]


def load_kernel(first, source, after, out, arrived):
    copy = pltpu.make_async_copy(source.at[pl.ds(first, out.shape[0])], out, arrived)
    copy.start()
    copy.wait()


def join_kernel(*refs):
    blocks, out = refs[1:-1], refs[-1]
    out[...] = jnp.concatenate([b[...].astype(F32) for b in blocks], axis=0).astype(BF16)


def loss_kernel(own, gather_levels, sum_levels, head_count, facts_ref, *refs):
    heads, (near_ref, far_ref, keep_ref, send_ref) = refs[:head_count], refs[head_count:]
    rows = jnp.concatenate([near_ref[...], far_ref[...]], axis=0)
    half, first, total, picked = rows.shape[0] // 2, 0, 0.0, 0.0
    for head_ref in heads:
        logits = lax.dot_general(
            head_ref[...], rows, (((1,), (1,)), ((), ())), preferred_element_type=F32
        )
        ids = lax.broadcasted_iota(I32, logits.shape, 0) + first
        total += jnp.sum(jnp.exp(logits), axis=0, keepdims=True)
        picked += jnp.sum(jnp.where(ids == facts_ref[0:1, :], logits, 0.0), axis=0, keepdims=True)
        first += head_ref.shape[0]
    holder = lax.broadcasted_iota(I32, (1, half), 1) >> log2(own)
    other = ((distance_at(holder, gather_levels[1:]) ^ distance_at(holder, sum_levels[1:])) & 1) == 1
    for row, values in enumerate((total, picked, facts_ref[1:2, :].astype(F32))):
        near, far = values[:, :half], values[:, half:]
        keep_ref[row : row + 1, :] = jnp.where(other, far, near)
        send_ref[row : row + 1, :] = jnp.where(other, near, far)


def add_lanes_kernel(came_count, keep_ref, *refs):
    total = keep_ref[...]
    for ref in refs[:came_count]:
        total += ref[...]
    outs = refs[came_count:]
    lanes = total.shape[1] // len(outs)
    for k, out in enumerate(outs):
        out[...] = total[:, k * lanes : (k + 1) * lanes]


def weight_kernel(tokens, came_count, segments_ref, train_ref, keep_ref, *refs):
    total = keep_ref[...]
    for ref in refs[:came_count]:
        total += ref[...]
    out = refs[came_count]
    own = out.shape[1]
    ref_loss = jnp.log(total[0:1]) - total[1:2]
    places = lax.axis_index(AXIS) * own + lax.broadcasted_iota(I32, (1, own), 1)
    same = (places + 1 < tokens) & (total[2:3].astype(I32) == segments_ref[...])
    out[...] = jnp.where(same, jax.nn.sigmoid(train_ref[...] - ref_loss), 0.0)


def on_device(
    hidden_units, residual, down_weight, final_gain, head_weight, targets, segments, train_loss
):
    own, width = residual.shape
    tokens, depth = hidden_units.shape
    vocab_rows = head_weight.shape[0]
    devices = lax.axis_size(AXIS)
    levels = levels_of(devices, 0)
    gather_levels = [*levels_of(devices, 1)[:-1], levels_of(devices, 0)[-1]]
    sum_levels = levels_of(devices, 1)

    half = (tokens // 2, width)
    gain = final_gain.reshape(-1, 128)
    sources = [hidden_units, targets[None, :], down_weight, residual, gain, segments[None, :], train_loss[None, :]]
    keep, send, facts, residual, gain, segments, train_loss = call(
        functools.partial(ffn_kernel, levels, gather_levels, own, vocab_rows),
        [(half, F32), (half, F32), ((2, tokens), I32)] + [(a.shape, a.dtype) for a in sources[3:]],
        *[pltpu.with_memory_space_constraint(a, pltpu.HBM) for a in sources],
        extra=bytes_of(down_weight),
        scratch=(
            pltpu.VMEM(hidden_units.shape, BF16),
            pltpu.VMEM((1, tokens), I32),
            pltpu.VMEM((CHUNKS, depth, width // CHUNKS), BF16),
            pltpu.SemaphoreType.DMA((CHUNKS,)),
            pltpu.SemaphoreType.DMA((6,)),
        ),
        specs=[IN_HBM] * 7,
    )
    came, rows = [swapped(send.astype(F16), levels[0][1])], tokens // 2
    for level in levels[1:-1]:
        size = len(level)
        rows //= size
        parts = (keep + sum(c.astype(F32) for c in came)).reshape(size, rows, width)
        keep = parts[0]
        came = [swapped(parts[k].astype(F16), level[k]) for k in range(1, size)]
    level = levels[-1]
    size = len(level)
    mine = keep + sum(c.astype(F32) for c in came)
    mine = mine + jnp.pad(residual.astype(F32), ((0, rows - own), (0, 0)))
    blocks = mine.astype(F16).reshape(size, own, width)
    came = [
        swapped(jnp.concatenate([blocks[place ^ k] for place in range(size)]), level[k])
        for k in range(1, size)
    ]
    head_hbm = pltpu.with_memory_space_constraint(head_weight, pltpu.HBM)

    def load(first, count, after):
        return call(
            functools.partial(load_kernel, first),
            [((count, width), BF16)],
            head_hbm,
            after,
            scratch=(pltpu.SemaphoreType.DMA,),
            specs=[IN_HBM, ANYWHERE],
        )[0]

    first = vocab_rows // 2
    heads = [load(0, first, mine)]
    heads[0], *came = lax.optimization_barrier((heads[0], *came))
    total = mine + sum(c.astype(F32) for c in came)
    states, block = call(
        functools.partial(norm_kernel, own),
        [((own, width), BF16), ((rows, width), BF16)],
        total,
        gain,
    )
    heads.append(load(first, vocab_rows - first, states))
    (hidden_states,) = call(copy_kernel, [(states.shape, BF16)], states)
    for level in gather_levels[-2:0:-1]:
        came = [swapped(block, distance) for distance in level[1:]]
        rows *= len(level)
        (block,) = call(
            join_kernel,
            [((rows, width), BF16)],
            heads[-1],
            block,
            *came,
            extra=bytes_of(block) * 8,
            specs=[ANYWHERE] + [WHOLE] * len(level),
        )
    far = swapped(block, gather_levels[0][1])

    keep, send = call(
        functools.partial(loss_kernel, own, gather_levels, sum_levels, len(heads)),
        [((3, tokens // 2), F32)] * 2,
        facts,
        *heads,
        block,
        far,
        extra=2 * bytes_of(block),
    )
    came, lanes = [swapped(send, sum_levels[0][1])], tokens // 2
    for level in sum_levels[1:]:
        lanes //= len(level)
        keep, *parts = call(
            functools.partial(add_lanes_kernel, len(came)), [((3, lanes), F32)] * len(level), keep, *came
        )
        came = [swapped(part, distance) for part, distance in zip(parts, level[1:])]
    (loss_weight,) = call(
        functools.partial(weight_kernel, tokens, len(came)), [((1, own), F32)], segments, train_loss, keep, *came
    )
    return (hidden_states, loss_weight.reshape(own))


def solution(mesh):
    placed = (
        P("groups", "stream"),
        P(("groups", "stream"), None),
        P("stream", None),
        P(),
        P("stream", None),
        P("groups"),
        P(("groups", "stream")),
        P(("groups", "stream")),
    )
    return jax.shard_map(
        on_device,
        mesh=mesh,
        in_specs=placed,
        out_specs=(P(("groups", "stream"), None), P(("groups", "stream"))),
        check_vma=False,
    )
```

time: 48.9 us -> 42.9 us (0.88)
  waiting for transfers between devices: 19.5 us -> 12.8 us
  starting transfers between devices: 18.5 us -> 17.6 us
  Pallas kernels: 10.1 us -> 10.9 us
    ppermute x14, waiting for transfers between devices: 19.5 us -> 12.8 us  [swapped(): lax.ppermute(block, AXIS, [(i, i ^ distance) for i in range(lax.axis_size...]
    ppermute x14, starting transfers between devices: 18.5 us -> 17.6 us  [swapped(): lax.ppermute(block, AXIS, [(i, i ^ distance) for i in range(lax.axis_size...]
    pallas_call x11 -> x10, Pallas kernels: 10.1 us -> 10.9 us  [call(): pl.pallas_call(body, out_shape=shapes, in_specs=specs or [WHOLE] * len(op...]
  transfers between devices with their start and end apart: 14 -> 14, of which waited for: 14 -> 12; matrix products, arithmetic and copies ran while one was open for 0% -> 0% of each run, Pallas kernels for 8% -> 12%
where the time goes in v3:
time: 42.9 us; the launch traced here: 42.6 us
  starting transfers between devices  17.6 us (41%)
  waiting for transfers between devices  12.8 us (30%)
  Pallas kernels  10.9 us (25%)
  between operations  0.73 us (2%)
    ppermute x14, starting transfers between devices, swapped(): lax.ppermute(block, AXIS, [(i, i ^ distance) for i in range(lax.axis_size...  17.6 us
    ppermute x14, waiting for transfers between devices, swapped(): lax.ppermute(block, AXIS, [(i, i ^ distance) for i in range(lax.axis_size...  12.8 us
    pallas_call x10, Pallas kernels, call(): pl.pallas_call(body, out_shape=shapes, in_specs=specs or [WHOLE] * len(op...  10.9 us
  transfers between devices with their start and end apart: 14, of which 12 were waited for; matrix products, arithmetic and copies ran while one was open for 0% of the time, Pallas kernels for 12%

profile of v3, /device:TPU:0, one launch (start us, length us, event | category | flops | bytes accessed | tf_op | source)
XLA Modules:
  0.0 42.6 jit_solution(14548198679491294863)
XLA Ops:
  0.6 2.6 %shard_map.95 = (f32[16,8192]{1,0:T(8,128)S(1)}, f32[16,8192]{1,0:T(8,128)S(1)}, s32[2,32]{1,0:T(2,128)S(1)}, bf16[2,8192]{1,0:T(2,128)(2,1)S(1)}, bf16[64,128]{...) custom-call(bf16[32,224]{1,0:T(8,128)(2,1)} %refs_0_.1, s32[1,32]{1,0:T(1,128)} %bitcast.6, ...), custom_call_target="tpu_custom_call" | custom-call | tf_op jit(solution)/shard_map/pallas_call | solution.py:48
  3.3 0.5 %collective-permute-start = (f16[16,8192]{1,0:T(8,128)(2,1)S(1)}, f16[16,8192]{1,0:T(8,128)(2,1)S(1)}, u32[]{:S(2)}, u32[]{:S(2)}) collective-permute-start(f16[16,8192]{1,0:T(8,128)(2,1)S(1)} %convert_element_type.27), channel_id=1, source_target_pairs={{0,1},{1,0},{2,3},{3,2},{4,5},{5,4},{6,7},{7,6},{8,9},{9,8},{10,11... | collective-permute-start | bytes 786440 | tf_op jit(solution)/shard_map/ppermute | solution.py:39
  3.8 1.2 %collective-permute-done = f16[16,8192]{1,0:T(8,128)(2,1)S(1)} collective-permute-done((f16[16,8192]{1,0:T(8,128)(2,1)S(1)}, f16[16,8192]{1,0:T(8,128)(2,1)S(1)}, u32[]{:S(2)}, u32[]{:S(2)}) %collective-permute-start) | collective-permute-done | bytes 262176 | tf_op jit(solution)/shard_map/ppermute | solution.py:39
  5.0 0.1 fusion.4
  5.1 3.0 %collective-permute-start.1 = (f16[4,8192]{1,0:T(4,128)(2,1)S(1)}, f16[4,8192]{1,0:T(4,128)(2,1)S(1)}, u32[]{:S(2)}, u32[]{:S(2)}) collective-permute-start(f16[4,8192]{1,0:T(4,128)(2,1)S(1)} %get-tuple-element.44), channel_id=1, source_target_pairs={{0,2},{1,3},{2,0},{3,1},{4,6},{5,7},{6,4},{7,5},{8,10},{9,11},{10,... | collective-permute-start | bytes 196616 | tf_op jit(solution)/shard_map/ppermute | solution.py:39
  8.1 1.5 %collective-permute-start.3 = (f16[4,8192]{1,0:T(4,128)(2,1)S(1)}, f16[4,8192]{1,0:T(4,128)(2,1)S(1)}, u32[]{:S(2)}, u32[]{:S(2)}) collective-permute-start(f16[4,8192]{1,0:T(4,128)(2,1)S(1)} %get-tuple-element.45), channel_id=1, source_target_pairs={{0,6},{1,7},{2,4},{3,5},{4,2},{5,3},{6,0},{7,1},{8,14},{9,15},{10,... | collective-permute-start | bytes 196616 | tf_op jit(solution)/shard_map/ppermute | solution.py:39
  9.7 1.6 %collective-permute-done.1 = f16[4,8192]{1,0:T(4,128)(2,1)S(1)} collective-permute-done((f16[4,8192]{1,0:T(4,128)(2,1)S(1)}, f16[4,8192]{1,0:T(4,128)(2,1)S(1)}, u32[]{:S(2)}, u32[]{:S(2)}) %collective-permute-start.1) | collective-permute-done | bytes 65568 | tf_op jit(solution)/shard_map/ppermute | solution.py:39
  11.3 2.5 %collective-permute-done.3 = f16[4,8192]{1,0:T(4,128)(2,1)S(1)} collective-permute-done((f16[4,8192]{1,0:T(4,128)(2,1)S(1)}, f16[4,8192]{1,0:T(4,128)(2,1)S(1)}, u32[]{:S(2)}, u32[]{:S(2)}) %collective-permute-start.3) | collective-permute-done | bytes 65568 | tf_op jit(solution)/shard_map/ppermute | solution.py:39
  13.8 0.1 collective-permute-done.2
  13.9 0.1 fusion.1
  14.1 2.7 %collective-permute-start.4 = (f16[4,8192]{1,0:T(4,128)(2,1)S(1)}, f16[4,8192]{1,0:T(4,128)(2,1)S(1)}, u32[]{:S(2)}, u32[]{:S(2)}) collective-permute-start(f16[4,8192]{1,0:T(4,128)(2,1)S(1)} %pad_maximum_fusion), channel_id=1, source_target_pairs={{0,8},{1,9},{2,10},{3,11},{4,12},{5,13},{6,14},{7,15},{8,0},{9,1},... | collective-permute-start | bytes 196616 | tf_op jit(solution)/shard_map/ppermute | solution.py:39
  16.8 2.2 %shard_map.96.refs_0_ = bf16[256,8192]{1,0:T(8,128)(2,1)S(1)} custom-call(bf16[512,8192]{1,0:T(8,128)(2,1)} %source.3, f32[4,8192]{1,0:T(4,128)S(1)} %get-tuple-element.41.after), custom_call_target="tpu_custom_call" | custom-call | tf_op jit(solution)/shard_map/pallas_call | solution.py:48
  19.0 0.4 collective-permute-done.4
  19.4 0.2 shard_map.97
  19.6 2.1 %collective-permute-start.7 = (bf16[4,8192]{1,0:T(4,128)(2,1)S(1)}, bf16[4,8192]{1,0:T(4,128)(2,1)S(1)}, u32[]{:S(2)}, u32[]{:S(2)}) collective-permute-start(bf16[4,8192]{1,0:T(4,128)(2,1)S(1)} %get-tuple-element.31.refs_1_), channel_id=1, source_target_pairs={{0,6},{1,7},{2,4},{3,5},{4,2},{5,3},{6,0},{7,1},{8,14},{9,15},{10,... | collective-permute-start | bytes 196616 | tf_op jit(solution)/shard_map/ppermute | solution.py:39
  21.7 1.2 %collective-permute-start.5 = (bf16[4,8192]{1,0:T(4,128)(2,1)S(1)}, bf16[4,8192]{1,0:T(4,128)(2,1)S(1)}, u32[]{:S(2)}, u32[]{:S(2)}) collective-permute-start(bf16[4,8192]{1,0:T(4,128)(2,1)S(1)} %get-tuple-element.31.refs_1_), channel_id=1, source_target_pairs={{0,3},{1,2},{2,1},{3,0},{4,7},{5,6},{6,5},{7,4},{8,11},{9,10},{10,... | collective-permute-start | bytes 196616 | tf_op jit(solution)/shard_map/ppermute | solution.py:39
  22.9 2.2 %shard_map.99.refs_0_.refs_1_ = bf16[256,8192]{1,0:T(8,128)(2,1)S(1)} custom-call(bf16[512,8192]{1,0:T(8,128)(2,1)} %source.3, bf16[2,8192]{1,0:T(2,128)(2,1)S(1)} %get-tuple-element.26.source.after), custom_call_target="tpu_custom_call" | custom-call | tf_op jit(solution)/shard_map/pallas_call | solution.py:48
  25.1 0.8 %collective-permute-done.6.refs_3_ = bf16[4,8192]{1,0:T(4,128)(2,1)S(1)} collective-permute-done((bf16[4,8192]{1,0:T(4,128)(2,1)S(1)}, bf16[4,8192]{1,0:T(4,128)(2,1)S(1)}, u32[]{:S(2)}, u32[]{:S(2)}) %collective-permute-start.6) | collective-permute-done | bytes 65568 | tf_op jit(solution)/shard_map/ppermute | solution.py:39
  26.1 1.2 %collective-permute-start.8 = (bf16[16,8192]{1,0:T(8,128)(2,1)S(1)}, bf16[16,8192]{1,0:T(8,128)(2,1)S(1)}, u32[]{:S(2)}, u32[]{:S(2)}) collective-permute-start(bf16[16,8192]{1,0:T(8,128)(2,1)S(1)} %shard_map.100.refs_2_), channel_id=1, source_target_pairs={{0,1},{1,0},{2,3},{3,2},{4,5},{5,4},{6,7},{7,6},{8,9},{9,8},{10,11... | collective-permute-start | bytes 786440 | tf_op jit(solution)/shard_map/ppermute | solution.py:39
  27.3 1.2 %collective-permute-done.8.refs_3_ = bf16[16,8192]{1,0:T(8,128)(2,1)S(1)} collective-permute-done((bf16[16,8192]{1,0:T(8,128)(2,1)S(1)}, bf16[16,8192]{1,0:T(8,128)(2,1)S(1)}, u32[]{:S(2)}, u32[]{:S(2)}) %collective-permute-start.8) | collective-permute-done | bytes 262176 | tf_op jit(solution)/shard_map/ppermute | solution.py:39
  28.5 2.4 %shard_map.101 = (f32[3,16]{1,0:T(4,128)S(1)}, f32[3,16]{1,0:T(4,128)S(1)}) custom-call(s32[2,32]{1,0:T(2,128)S(1)} %get-tuple-element.29.facts_ref, bf16[256,8192]{1,0:T(8,128)(2,1)S(1)} %shard_map.96.refs_0_, bf16[256,8192]{1,0:T(8,128)(2,1)S(1)} %shard_map.99.refs_0_.refs_1_, bf16[16,8192]{1,0:T(8,128)(2,1)S(1)} %shard_map.100.refs_2_, ...), custom_call_target="tpu_custom_call" | custom-call | tf_op jit(solution)/shard_map/pallas_call | solution.py:48
  30.9 0.4 collective-permute-start.9
  31.2 0.6 %shard_map.98 = bf16[2,8192]{1,0:T(2,128)(2,1)} custom-call(bf16[2,8192]{1,0:T(2,128)(2,1)S(1)} %get-tuple-element.26.source.after), custom_call_target="tpu_custom_call" | custom-call | tf_op jit(solution)/shard_map/pallas_call | solution.py:48
  31.9 0.2 collective-permute-done.9.refs_0_
  32.1 1.3 %collective-permute-start.10 = (f32[3,4]{1,0:T(4,128)S(1)}, f32[3,4]{1,0:T(4,128)S(1)}, u32[]{:S(2)}, u32[]{:S(2)}) collective-permute-start(f32[3,4]{1,0:T(4,128)S(1)} %get-tuple-element.35), channel_id=1, source_target_pairs={{0,3},{1,2},{2,1},{3,0},{4,7},{5,6},{6,5},{7,4},{8,11},{9,10},{10,... | collective-permute-start | bytes 152 | tf_op jit(solution)/shard_map/ppermute | solution.py:39
  33.5 0.1 collective-permute-start.11
  33.6 1.7 %collective-permute-start.12 = (f32[3,4]{1,0:T(4,128)S(1)}, f32[3,4]{1,0:T(4,128)S(1)}, u32[]{:S(2)}, u32[]{:S(2)}) collective-permute-start(f32[3,4]{1,0:T(4,128)S(1)} %get-tuple-element.37), channel_id=1, source_target_pairs={{0,6},{1,7},{2,4},{3,5},{4,2},{5,3},{6,0},{7,1},{8,14},{9,15},{10,... | collective-permute-start | bytes 152 | tf_op jit(solution)/shard_map/ppermute | solution.py:39
  35.3 1.1 %collective-permute-done.11.refs_1_ = f32[3,4]{1,0:T(4,128)S(1)} collective-permute-done((f32[3,4]{1,0:T(4,128)S(1)}, f32[3,4]{1,0:T(4,128)S(1)}, u32[]{:S(2)}, u32[]{:S(2)}) %collective-permute-start.11) | collective-permute-done | bytes 80 | tf_op jit(solution)/shard_map/ppermute | solution.py:39
  36.5 1.6 %collective-permute-done.12.refs_2_ = f32[3,4]{1,0:T(4,128)S(1)} collective-permute-done((f32[3,4]{1,0:T(4,128)S(1)}, f32[3,4]{1,0:T(4,128)S(1)}, u32[]{:S(2)}, u32[]{:S(2)}) %collective-permute-start.12) | collective-permute-done | bytes 80 | tf_op jit(solution)/shard_map/ppermute | solution.py:39
  38.2 1.8 %collective-permute-start.13 = (f32[3,2]{1,0:T(4,128)S(1)}, f32[3,2]{1,0:T(4,128)S(1)}, u32[]{:S(2)}, u32[]{:S(2)}) collective-permute-start(f32[3,2]{1,0:T(4,128)S(1)} %get-tuple-element.39), channel_id=1, source_target_pairs={{0,9},{1,8},{2,11},{3,10},{4,13},{5,12},{6,15},{7,14},{8,1},{9,0},... | collective-permute-start | bytes 80 | tf_op jit(solution)/shard_map/ppermute | solution.py:39
  40.0 2.1 %collective-permute-done.13.refs_0_ = f32[3,2]{1,0:T(4,128)S(1)} collective-permute-done((f32[3,2]{1,0:T(4,128)S(1)}, f32[3,2]{1,0:T(4,128)S(1)}, u32[]{:S(2)}, u32[]{:S(2)}) %collective-permute-start.13) | collective-permute-done | bytes 56 | tf_op jit(solution)/shard_map/ppermute | solution.py:39
  42.1 0.5 %shard_map.104 = f32[1,2]{1,0:T(1,128)} custom-call(s32[1,2]{1,0:T(1,128)S(1)} %get-tuple-element.27.segments_ref, f32[1,2]{1,0:T(1,128)S(1)} %get-tuple-element.28.train_ref, f32[3,2]{1,0:T(4,128)S(1)} %get-tuple-element.38.keep_ref, f32[3,2]{1,0:T(4,128)S(1)} %collective-permute-done.13.refs_0_), custom_call_target="tpu_custom_call" | custom-call | tf_op jit(solution)/shard_map/pallas_call | solution.py:48
  (13 shorter events, 0.6 us)
Async XLA Ops:
  3.3 1.7 %collective-permute-start = (f16[16,8192]{1,0:T(8,128)(2,1)S(1)}, f16[16,8192]{1,0:T(8,128)(2,1)S(1)}, u32[]{:S(2)}, u32[]{:S(2)}) collective-permute-start(f16[16,8192]{1,0:T(8,128)(2,1)S(1)} %convert_element_type.27), channel_id=1, source_target_pairs={{0,1},{1,0},{2,3},{3,2},{4,5},{5,4},{6,7},{7,6},{8,9},{9,8},{10,11... | collective-permute-start | bytes 786440 | tf_op jit(solution)/shard_map/ppermute | solution.py:39
  5.1 6.2 %collective-permute-start.1 = (f16[4,8192]{1,0:T(4,128)(2,1)S(1)}, f16[4,8192]{1,0:T(4,128)(2,1)S(1)}, u32[]{:S(2)}, u32[]{:S(2)}) collective-permute-start(f16[4,8192]{1,0:T(4,128)(2,1)S(1)} %get-tuple-element.44), channel_id=1, source_target_pairs={{0,2},{1,3},{2,0},{3,1},{4,6},{5,7},{6,4},{7,5},{8,10},{9,11},{10,... | collective-permute-start | bytes 196616 | tf_op jit(solution)/shard_map/ppermute | solution.py:39
  8.1 5.7 %collective-permute-start.3 = (f16[4,8192]{1,0:T(4,128)(2,1)S(1)}, f16[4,8192]{1,0:T(4,128)(2,1)S(1)}, u32[]{:S(2)}, u32[]{:S(2)}) collective-permute-start(f16[4,8192]{1,0:T(4,128)(2,1)S(1)} %get-tuple-element.45), channel_id=1, source_target_pairs={{0,6},{1,7},{2,4},{3,5},{4,2},{5,3},{6,0},{7,1},{8,14},{9,15},{10,... | collective-permute-start | bytes 196616 | tf_op jit(solution)/shard_map/ppermute | solution.py:39
  9.6 4.3 %collective-permute-start.2 = (f16[4,8192]{1,0:T(4,128)(2,1)S(1)}, f16[4,8192]{1,0:T(4,128)(2,1)S(1)}, u32[]{:S(2)}, u32[]{:S(2)}) collective-permute-start(f16[4,8192]{1,0:T(4,128)(2,1)S(1)} %get-tuple-element.46), channel_id=1, source_target_pairs={{0,4},{1,5},{2,6},{3,7},{4,0},{5,1},{6,2},{7,3},{8,12},{9,13},{10,... | collective-permute-start | bytes 196616 | tf_op jit(solution)/shard_map/ppermute | solution.py:39
  14.1 5.2 %collective-permute-start.4 = (f16[4,8192]{1,0:T(4,128)(2,1)S(1)}, f16[4,8192]{1,0:T(4,128)(2,1)S(1)}, u32[]{:S(2)}, u32[]{:S(2)}) collective-permute-start(f16[4,8192]{1,0:T(4,128)(2,1)S(1)} %pad_maximum_fusion), channel_id=1, source_target_pairs={{0,8},{1,9},{2,10},{3,11},{4,12},{5,13},{6,14},{7,15},{8,0},{9,1},... | collective-permute-start | bytes 196616 | tf_op jit(solution)/shard_map/ppermute | solution.py:39
  19.6 5.5 %collective-permute-start.7 = (bf16[4,8192]{1,0:T(4,128)(2,1)S(1)}, bf16[4,8192]{1,0:T(4,128)(2,1)S(1)}, u32[]{:S(2)}, u32[]{:S(2)}) collective-permute-start(bf16[4,8192]{1,0:T(4,128)(2,1)S(1)} %get-tuple-element.31.refs_1_), channel_id=1, source_target_pairs={{0,6},{1,7},{2,4},{3,5},{4,2},{5,3},{6,0},{7,1},{8,14},{9,15},{10,... | collective-permute-start | bytes 196616 | tf_op jit(solution)/shard_map/ppermute | solution.py:39
  21.7 4.2 %collective-permute-start.6 = (bf16[4,8192]{1,0:T(4,128)(2,1)S(1)}, bf16[4,8192]{1,0:T(4,128)(2,1)S(1)}, u32[]{:S(2)}, u32[]{:S(2)}) collective-permute-start(bf16[4,8192]{1,0:T(4,128)(2,1)S(1)} %get-tuple-element.31.refs_1_), channel_id=1, source_target_pairs={{0,5},{1,4},{2,7},{3,6},{4,1},{5,0},{6,3},{7,2},{8,13},{9,12},{10,... | collective-permute-start | bytes 196616 | tf_op jit(solution)/shard_map/ppermute | solution.py:39
  21.7 4.3 %collective-permute-start.5 = (bf16[4,8192]{1,0:T(4,128)(2,1)S(1)}, bf16[4,8192]{1,0:T(4,128)(2,1)S(1)}, u32[]{:S(2)}, u32[]{:S(2)}) collective-permute-start(bf16[4,8192]{1,0:T(4,128)(2,1)S(1)} %get-tuple-element.31.refs_1_), channel_id=1, source_target_pairs={{0,3},{1,2},{2,1},{3,0},{4,7},{5,6},{6,5},{7,4},{8,11},{9,10},{10,... | collective-permute-start | bytes 196616 | tf_op jit(solution)/shard_map/ppermute | solution.py:39
  26.1 2.4 %collective-permute-start.8 = (bf16[16,8192]{1,0:T(8,128)(2,1)S(1)}, bf16[16,8192]{1,0:T(8,128)(2,1)S(1)}, u32[]{:S(2)}, u32[]{:S(2)}) collective-permute-start(bf16[16,8192]{1,0:T(8,128)(2,1)S(1)} %shard_map.100.refs_2_), channel_id=1, source_target_pairs={{0,1},{1,0},{2,3},{3,2},{4,5},{5,4},{6,7},{7,6},{8,9},{9,8},{10,11... | collective-permute-start | bytes 786440 | tf_op jit(solution)/shard_map/ppermute | solution.py:39
  30.9 1.2 %collective-permute-start.9 = (f32[3,16]{1,0:T(4,128)S(1)}, f32[3,16]{1,0:T(4,128)S(1)}, u32[]{:S(2)}, u32[]{:S(2)}) collective-permute-start(f32[3,16]{1,0:T(4,128)S(1)} %get-tuple-element.33), channel_id=1, source_target_pairs={{0,1},{1,0},{2,3},{3,2},{4,5},{5,4},{6,7},{7,6},{8,9},{9,8},{10,11... | collective-permute-start | bytes 584 | tf_op jit(solution)/shard_map/ppermute | solution.py:39
  32.1 3.2 %collective-permute-start.10 = (f32[3,4]{1,0:T(4,128)S(1)}, f32[3,4]{1,0:T(4,128)S(1)}, u32[]{:S(2)}, u32[]{:S(2)}) collective-permute-start(f32[3,4]{1,0:T(4,128)S(1)} %get-tuple-element.35), channel_id=1, source_target_pairs={{0,3},{1,2},{2,1},{3,0},{4,7},{5,6},{6,5},{7,4},{8,11},{9,10},{10,... | collective-permute-start | bytes 152 | tf_op jit(solution)/shard_map/ppermute | solution.py:39
  33.5 3.0 %collective-permute-start.11 = (f32[3,4]{1,0:T(4,128)S(1)}, f32[3,4]{1,0:T(4,128)S(1)}, u32[]{:S(2)}, u32[]{:S(2)}) collective-permute-start(f32[3,4]{1,0:T(4,128)S(1)} %get-tuple-element.36), channel_id=1, source_target_pairs={{0,5},{1,4},{2,7},{3,6},{4,1},{5,0},{6,3},{7,2},{8,13},{9,12},{10,... | collective-permute-start | bytes 152 | tf_op jit(solution)/shard_map/ppermute | solution.py:39
  33.6 4.5 %collective-permute-start.12 = (f32[3,4]{1,0:T(4,128)S(1)}, f32[3,4]{1,0:T(4,128)S(1)}, u32[]{:S(2)}, u32[]{:S(2)}) collective-permute-start(f32[3,4]{1,0:T(4,128)S(1)} %get-tuple-element.37), channel_id=1, source_target_pairs={{0,6},{1,7},{2,4},{3,5},{4,2},{5,3},{6,0},{7,1},{8,14},{9,15},{10,... | collective-permute-start | bytes 152 | tf_op jit(solution)/shard_map/ppermute | solution.py:39
  38.2 3.9 %collective-permute-start.13 = (f32[3,2]{1,0:T(4,128)S(1)}, f32[3,2]{1,0:T(4,128)S(1)}, u32[]{:S(2)}, u32[]{:S(2)}) collective-permute-start(f32[3,2]{1,0:T(4,128)S(1)} %get-tuple-element.39), channel_id=1, source_target_pairs={{0,9},{1,8},{2,11},{3,10},{4,13},{5,12},{6,15},{7,14},{8,1},{9,0},... | collective-permute-start | bytes 80 | tf_op jit(solution)/shard_map/ppermute | solution.py:39

commit v4 on v3

--- a/solution.py
+++ b/solution.py
@@ -117,8 +117,13 @@
     facts_ref[1:2, :] = following
 
 
-def norm_kernel(own, total_ref, gain_ref, states_ref, normed_ref):
-    states = total_ref[...].astype(BF16)
+def norm_kernel(own, size, gain_ref, mine_ref, *refs):
+    came, (states_ref, normed_ref) = refs[: size - 1], refs[size - 1 :]
+    total = mine_ref[...]
+    for k in range(1, size):
+        order = [place ^ k for place in range(size)]
+        total += jnp.concatenate([came[k - 1][p * own : (p + 1) * own, :] for p in order], axis=0)
+    states = total.astype(BF16)
     states_ref[...] = states[:own]
     values = states.astype(F32)
     scale = lax.rsqrt(jnp.mean(values * values, axis=1, keepdims=True) + 1e-05)
@@ -127,7 +132,7 @@
         normed_ref[:, at] = (values[:, at] * scale * gain_ref[c : c + 1, :].astype(F32)).astype(BF16)
 
 
-def copy_kernel(source, out):
+def copy_kernel(source, after, out):
     out[...] = source[...]
 
 
@@ -218,16 +223,12 @@
         rows //= size
         parts = (keep + sum(c.astype(F32) for c in came)).reshape(size, rows, width)
         keep = parts[0]
-        came = [swapped(parts[k].astype(F16), level[k]) for k in range(1, size)]
+        came = [swapped(parts[k].astype(F16), level[k]) for k in range(size - 1, 0, -1)]
     level = levels[-1]
     size = len(level)
     mine = keep + sum(c.astype(F32) for c in came)
     mine = mine + jnp.pad(residual.astype(F32), ((0, rows - own), (0, 0)))
-    blocks = mine.astype(F16).reshape(size, own, width)
-    came = [
-        swapped(jnp.concatenate([blocks[place ^ k] for place in range(size)]), level[k])
-        for k in range(1, size)
-    ]
+    came = [swapped(mine.astype(F16), level[k]) for k in range(1, size)]
     head_hbm = pltpu.with_memory_space_constraint(head_weight, pltpu.HBM)
 
     def load(first, count, after):
@@ -243,15 +244,14 @@
     first = vocab_rows // 2
     heads = [load(0, first, mine)]
     heads[0], *came = lax.optimization_barrier((heads[0], *came))
-    total = mine + sum(c.astype(F32) for c in came)
     states, block = call(
-        functools.partial(norm_kernel, own),
+        functools.partial(norm_kernel, own, size),
         [((own, width), BF16), ((rows, width), BF16)],
-        total,
         gain,
+        mine,
+        *[c.astype(F32) for c in came],
     )
     heads.append(load(first, vocab_rows - first, states))
-    (hidden_states,) = call(copy_kernel, [(states.shape, BF16)], states)
     for level in gather_levels[-2:0:-1]:
         came = [swapped(block, distance) for distance in level[1:]]
         rows *= len(level)
@@ -281,7 +281,12 @@
         keep, *parts = call(
             functools.partial(add_lanes_kernel, len(came)), [((3, lanes), F32)] * len(level), keep, *came
         )
-        came = [swapped(part, distance) for part, distance in zip(parts, level[1:])]
+        sends = list(zip(parts, level[1:]))
+        came = [swapped(*send) for send in sends[-1:] + sends[:-1]]
+        if level is sum_levels[1]:
+            (hidden_states,) = call(
+                copy_kernel, [(states.shape, BF16)], states, came[0], specs=[WHOLE, ANYWHERE]
+            )
     (loss_weight,) = call(
         functools.partial(weight_kernel, tokens, len(came)), [((1, own), F32)], segments, train_loss, keep, *came
     )

time: 42.9 us -> 41.5 us (0.967)
  waiting for transfers between devices: 12.8 us -> 11.4 us
    ppermute x14, waiting for transfers between devices: 12.8 us -> 11.4 us  [swapped(): lax.ppermute(block, AXIS, [(i, i ^ distance) for i in range(lax.axis_size...]
where the time goes in v4:
time: 41.5 us; the launch traced here: 41.1 us
  starting transfers between devices  17.7 us (43%)
  waiting for transfers between devices  11.4 us (27%)
  Pallas kernels  11 us (27%)
  between operations  0.71 us (2%)
    ppermute x14, starting transfers between devices, swapped(): lax.ppermute(block, AXIS, [(i, i ^ distance) for i in range(lax.axis_size...  17.7 us
    ppermute x14, waiting for transfers between devices, swapped(): lax.ppermute(block, AXIS, [(i, i ^ distance) for i in range(lax.axis_size...  11.4 us
    pallas_call x10, Pallas kernels, call(): pl.pallas_call(body, out_shape=shapes, in_specs=specs or [WHOLE] * len(op...  11 us
  transfers between devices with their start and end apart: 14, of which 12 were waited for; matrix products, arithmetic and copies ran while one was open for 0% of the time, Pallas kernels for 12%

profile of v4, /device:TPU:0, one launch (start us, length us, event | category | flops | bytes accessed | tf_op | source)
XLA Modules:
  0.0 41.1 jit_solution(3606361838125630447)
XLA Ops:
  0.6 2.6 %shard_map.95 = (f32[16,8192]{1,0:T(8,128)S(1)}, f32[16,8192]{1,0:T(8,128)S(1)}, s32[2,32]{1,0:T(2,128)S(1)}, bf16[2,8192]{1,0:T(2,128)(2,1)S(1)}, bf16[64,128]{...) custom-call(bf16[32,224]{1,0:T(8,128)(2,1)} %refs_0_.1, s32[1,32]{1,0:T(1,128)} %bitcast.6, ...), custom_call_target="tpu_custom_call" | custom-call | tf_op jit(solution)/shard_map/pallas_call | solution.py:48
  3.3 0.5 %collective-permute-start = (f16[16,8192]{1,0:T(8,128)(2,1)S(1)}, f16[16,8192]{1,0:T(8,128)(2,1)S(1)}, u32[]{:S(2)}, u32[]{:S(2)}) collective-permute-start(f16[16,8192]{1,0:T(8,128)(2,1)S(1)} %convert_element_type.27), channel_id=1, source_target_pairs={{0,1},{1,0},{2,3},{3,2},{4,5},{5,4},{6,7},{7,6},{8,9},{9,8},{10,11... | collective-permute-start | bytes 786440 | tf_op jit(solution)/shard_map/ppermute | solution.py:39
  3.8 1.2 %collective-permute-done = f16[16,8192]{1,0:T(8,128)(2,1)S(1)} collective-permute-done((f16[16,8192]{1,0:T(8,128)(2,1)S(1)}, f16[16,8192]{1,0:T(8,128)(2,1)S(1)}, u32[]{:S(2)}, u32[]{:S(2)}) %collective-permute-start) | collective-permute-done | bytes 262176 | tf_op jit(solution)/shard_map/ppermute | solution.py:39
  5.1 4.0 %collective-permute-start.1 = (f16[4,8192]{1,0:T(4,128)(2,1)S(1)}, f16[4,8192]{1,0:T(4,128)(2,1)S(1)}, u32[]{:S(2)}, u32[]{:S(2)}) collective-permute-start(f16[4,8192]{1,0:T(4,128)(2,1)S(1)} %get-tuple-element.44), channel_id=1, source_target_pairs={{0,6},{1,7},{2,4},{3,5},{4,2},{5,3},{6,0},{7,1},{8,14},{9,15},{10,... | collective-permute-start | bytes 196616 | tf_op jit(solution)/shard_map/ppermute | solution.py:39
  9.1 0.5 %collective-permute-start.3 = (f16[4,8192]{1,0:T(4,128)(2,1)S(1)}, f16[4,8192]{1,0:T(4,128)(2,1)S(1)}, u32[]{:S(2)}, u32[]{:S(2)}) collective-permute-start(f16[4,8192]{1,0:T(4,128)(2,1)S(1)} %get-tuple-element.45), channel_id=1, source_target_pairs={{0,2},{1,3},{2,0},{3,1},{4,6},{5,7},{6,4},{7,5},{8,10},{9,11},{10,... | collective-permute-start | bytes 196616 | tf_op jit(solution)/shard_map/ppermute | solution.py:39
  9.6 0.1 collective-permute-start.2
  9.7 1.8 %collective-permute-done.1 = f16[4,8192]{1,0:T(4,128)(2,1)S(1)} collective-permute-done((f16[4,8192]{1,0:T(4,128)(2,1)S(1)}, f16[4,8192]{1,0:T(4,128)(2,1)S(1)}, u32[]{:S(2)}, u32[]{:S(2)}) %collective-permute-start.1) | collective-permute-done | bytes 65568 | tf_op jit(solution)/shard_map/ppermute | solution.py:39
  11.5 1.9 %collective-permute-done.3 = f16[4,8192]{1,0:T(4,128)(2,1)S(1)} collective-permute-done((f16[4,8192]{1,0:T(4,128)(2,1)S(1)}, f16[4,8192]{1,0:T(4,128)(2,1)S(1)}, u32[]{:S(2)}, u32[]{:S(2)}) %collective-permute-start.3) | collective-permute-done | bytes 65568 | tf_op jit(solution)/shard_map/ppermute | solution.py:39
  13.4 0.5 %collective-permute-done.2 = f16[4,8192]{1,0:T(4,128)(2,1)S(1)} collective-permute-done((f16[4,8192]{1,0:T(4,128)(2,1)S(1)}, f16[4,8192]{1,0:T(4,128)(2,1)S(1)}, u32[]{:S(2)}, u32[]{:S(2)}) %collective-permute-start.2) | collective-permute-done | bytes 65568 | tf_op jit(solution)/shard_map/ppermute | solution.py:39
  13.9 0.1 fusion.1
  14.0 2.7 %collective-permute-start.4 = (f16[4,8192]{1,0:T(4,128)(2,1)S(1)}, f16[4,8192]{1,0:T(4,128)(2,1)S(1)}, u32[]{:S(2)}, u32[]{:S(2)}) collective-permute-start(f16[4,8192]{1,0:T(4,128)(2,1)S(1)} %get-tuple-element.40), channel_id=1, source_target_pairs={{0,8},{1,9},{2,10},{3,11},{4,12},{5,13},{6,14},{7,15},{8,0},{9,1},... | collective-permute-start | bytes 196616 | tf_op jit(solution)/shard_map/ppermute | solution.py:39
  16.6 2.2 %shard_map.96.refs_0_ = bf16[256,8192]{1,0:T(8,128)(2,1)S(1)} custom-call(bf16[512,8192]{1,0:T(8,128)(2,1)} %source.3, f32[4,8192]{1,0:T(4,128)S(1)} %get-tuple-element.41.after.mine_ref), custom_call_target="tpu_custom_call" | custom-call | tf_op jit(solution)/shard_map/pallas_call | solution.py:48
  18.8 1.1 %collective-permute-done.4 = f16[4,8192]{1,0:T(4,128)(2,1)S(1)} collective-permute-done((f16[4,8192]{1,0:T(4,128)(2,1)S(1)}, f16[4,8192]{1,0:T(4,128)(2,1)S(1)}, u32[]{:S(2)}, u32[]{:S(2)}) %collective-permute-start.4) | collective-permute-done | bytes 65568 | tf_op jit(solution)/shard_map/ppermute | solution.py:39
  19.9 0.3 shard_map.97
  20.2 0.8 %collective-permute-start.7 = (bf16[4,8192]{1,0:T(4,128)(2,1)S(1)}, bf16[4,8192]{1,0:T(4,128)(2,1)S(1)}, u32[]{:S(2)}, u32[]{:S(2)}) collective-permute-start(bf16[4,8192]{1,0:T(4,128)(2,1)S(1)} %get-tuple-element.29.refs_1_), channel_id=1, source_target_pairs={{0,6},{1,7},{2,4},{3,5},{4,2},{5,3},{6,0},{7,1},{8,14},{9,15},{10,... | collective-permute-start | bytes 196616 | tf_op jit(solution)/shard_map/ppermute | solution.py:39
  21.0 2.4 %collective-permute-start.5 = (bf16[4,8192]{1,0:T(4,128)(2,1)S(1)}, bf16[4,8192]{1,0:T(4,128)(2,1)S(1)}, u32[]{:S(2)}, u32[]{:S(2)}) collective-permute-start(bf16[4,8192]{1,0:T(4,128)(2,1)S(1)} %get-tuple-element.29.refs_1_), channel_id=1, source_target_pairs={{0,3},{1,2},{2,1},{3,0},{4,7},{5,6},{6,5},{7,4},{8,11},{9,10},{10,... | collective-permute-start | bytes 196616 | tf_op jit(solution)/shard_map/ppermute | solution.py:39
  23.5 2.2 %shard_map.98.refs_0_.refs_1_ = bf16[256,8192]{1,0:T(8,128)(2,1)S(1)} custom-call(bf16[512,8192]{1,0:T(8,128)(2,1)} %source.3, bf16[2,8192]{1,0:T(2,128)(2,1)S(1)} %get-tuple-element.26.after.source), custom_call_target="tpu_custom_call" | custom-call | tf_op jit(solution)/shard_map/pallas_call | solution.py:48
  25.8 0.4 collective-permute-done.5.refs_2_
  26.2 0.9 %collective-permute-start.8 = (bf16[16,8192]{1,0:T(8,128)(2,1)S(1)}, bf16[16,8192]{1,0:T(8,128)(2,1)S(1)}, u32[]{:S(2)}, u32[]{:S(2)}) collective-permute-start(bf16[16,8192]{1,0:T(8,128)(2,1)S(1)} %shard_map.99.refs_2_), channel_id=1, source_target_pairs={{0,1},{1,0},{2,3},{3,2},{4,5},{5,4},{6,7},{7,6},{8,9},{9,8},{10,11... | collective-permute-start | bytes 786440 | tf_op jit(solution)/shard_map/ppermute | solution.py:39
  27.1 1.2 %collective-permute-done.8.refs_3_ = bf16[16,8192]{1,0:T(8,128)(2,1)S(1)} collective-permute-done((bf16[16,8192]{1,0:T(8,128)(2,1)S(1)}, bf16[16,8192]{1,0:T(8,128)(2,1)S(1)}, u32[]{:S(2)}, u32[]{:S(2)}) %collective-permute-start.8) | collective-permute-done | bytes 262176 | tf_op jit(solution)/shard_map/ppermute | solution.py:39
  28.2 2.4 %shard_map.100 = (f32[3,16]{1,0:T(4,128)S(1)}, f32[3,16]{1,0:T(4,128)S(1)}) custom-call(s32[2,32]{1,0:T(2,128)S(1)} %get-tuple-element.27.facts_ref, bf16[256,8192]{1,0:T(8,128)(2,1)S(1)} %shard_map.96.refs_0_, bf16[256,8192]{1,0:T(8,128)(2,1)S(1)} %shard_map.98.refs_0_.refs_1_, bf16[16,8192]{1,0:T(8,128)(2,1)S(1)} %shard_map.99.refs_2_, ...), custom_call_target="tpu_custom_call" | custom-call | tf_op jit(solution)/shard_map/pallas_call | solution.py:48
  30.6 0.4 collective-permute-start.9
  31.0 0.8 %collective-permute-done.9.refs_0_ = f32[3,16]{1,0:T(4,128)S(1)} collective-permute-done((f32[3,16]{1,0:T(4,128)S(1)}, f32[3,16]{1,0:T(4,128)S(1)}, u32[]{:S(2)}, u32[]{:S(2)}) %collective-permute-start.9) | collective-permute-done | bytes 224 | tf_op jit(solution)/shard_map/ppermute | solution.py:39
  31.9 0.6 %collective-permute-start.10 = (f32[3,4]{1,0:T(4,128)S(1)}, f32[3,4]{1,0:T(4,128)S(1)}, u32[]{:S(2)}, u32[]{:S(2)}) collective-permute-start(f32[3,4]{1,0:T(4,128)S(1)} %get-tuple-element.32), channel_id=1, source_target_pairs={{0,6},{1,7},{2,4},{3,5},{4,2},{5,3},{6,0},{7,1},{8,14},{9,15},{10,... | collective-permute-start | bytes 152 | tf_op jit(solution)/shard_map/ppermute | solution.py:39
  32.5 1.1 %collective-permute-start.11 = (f32[3,4]{1,0:T(4,128)S(1)}, f32[3,4]{1,0:T(4,128)S(1)}, u32[]{:S(2)}, u32[]{:S(2)}) collective-permute-start(f32[3,4]{1,0:T(4,128)S(1)} %get-tuple-element.36), channel_id=1, source_target_pairs={{0,3},{1,2},{2,1},{3,0},{4,7},{5,6},{6,5},{7,4},{8,11},{9,10},{10,... | collective-permute-start | bytes 152 | tf_op jit(solution)/shard_map/ppermute | solution.py:39
  33.6 1.5 %collective-permute-start.12 = (f32[3,4]{1,0:T(4,128)S(1)}, f32[3,4]{1,0:T(4,128)S(1)}, u32[]{:S(2)}, u32[]{:S(2)}) collective-permute-start(f32[3,4]{1,0:T(4,128)S(1)} %get-tuple-element.37), channel_id=1, source_target_pairs={{0,5},{1,4},{2,7},{3,6},{4,1},{5,0},{6,3},{7,2},{8,13},{9,12},{10,... | collective-permute-start | bytes 152 | tf_op jit(solution)/shard_map/ppermute | solution.py:39
  35.1 1.3 %collective-permute-done.10.after.refs_0_ = f32[3,4]{1,0:T(4,128)S(1)} collective-permute-done((f32[3,4]{1,0:T(4,128)S(1)}, f32[3,4]{1,0:T(4,128)S(1)}, u32[]{:S(2)}, u32[]{:S(2)}) %collective-permute-start.10) | collective-permute-done | bytes 80 | tf_op jit(solution)/shard_map/ppermute | solution.py:39
  36.4 0.2 collective-permute-done.12.refs_2_
  36.7 2.1 %collective-permute-start.13 = (f32[3,2]{1,0:T(4,128)S(1)}, f32[3,2]{1,0:T(4,128)S(1)}, u32[]{:S(2)}, u32[]{:S(2)}) collective-permute-start(f32[3,2]{1,0:T(4,128)S(1)} %get-tuple-element.39), channel_id=1, source_target_pairs={{0,9},{1,8},{2,11},{3,10},{4,13},{5,12},{6,15},{7,14},{8,1},{9,0},... | collective-permute-start | bytes 80 | tf_op jit(solution)/shard_map/ppermute | solution.py:39
  38.8 0.6 %shard_map.102 = bf16[2,8192]{1,0:T(2,128)(2,1)} custom-call(bf16[2,8192]{1,0:T(2,128)(2,1)S(1)} %get-tuple-element.26.after.source, f32[3,4]{1,0:T(4,128)S(1)} %collective-permute-done.10.after.refs_0_), custom_call_target="tpu_custom_call" | custom-call | tf_op jit(solution)/shard_map/pallas_call | solution.py:48
  39.4 1.2 %collective-permute-done.13.refs_0_ = f32[3,2]{1,0:T(4,128)S(1)} collective-permute-done((f32[3,2]{1,0:T(4,128)S(1)}, f32[3,2]{1,0:T(4,128)S(1)}, u32[]{:S(2)}, u32[]{:S(2)}) %collective-permute-start.13) | collective-permute-done | bytes 56 | tf_op jit(solution)/shard_map/ppermute | solution.py:39
  40.6 0.5 %shard_map.104 = f32[1,2]{1,0:T(1,128)} custom-call(s32[1,2]{1,0:T(1,128)S(1)} %get-tuple-element.33.segments_ref, f32[1,2]{1,0:T(1,128)S(1)} %get-tuple-element.34.train_ref, f32[3,2]{1,0:T(4,128)S(1)} %get-tuple-element.38.keep_ref, f32[3,2]{1,0:T(4,128)S(1)} %collective-permute-done.13.refs_0_), custom_call_target="tpu_custom_call" | custom-call | tf_op jit(solution)/shard_map/pallas_call | solution.py:48
  (11 shorter events, 0.5 us)
Async XLA Ops:
  3.3 1.7 %collective-permute-start = (f16[16,8192]{1,0:T(8,128)(2,1)S(1)}, f16[16,8192]{1,0:T(8,128)(2,1)S(1)}, u32[]{:S(2)}, u32[]{:S(2)}) collective-permute-start(f16[16,8192]{1,0:T(8,128)(2,1)S(1)} %convert_element_type.27), channel_id=1, source_target_pairs={{0,1},{1,0},{2,3},{3,2},{4,5},{5,4},{6,7},{7,6},{8,9},{9,8},{10,11... | collective-permute-start | bytes 786440 | tf_op jit(solution)/shard_map/ppermute | solution.py:39
  5.1 6.4 %collective-permute-start.1 = (f16[4,8192]{1,0:T(4,128)(2,1)S(1)}, f16[4,8192]{1,0:T(4,128)(2,1)S(1)}, u32[]{:S(2)}, u32[]{:S(2)}) collective-permute-start(f16[4,8192]{1,0:T(4,128)(2,1)S(1)} %get-tuple-element.44), channel_id=1, source_target_pairs={{0,6},{1,7},{2,4},{3,5},{4,2},{5,3},{6,0},{7,1},{8,14},{9,15},{10,... | collective-permute-start | bytes 196616 | tf_op jit(solution)/shard_map/ppermute | solution.py:39
  9.1 4.3 %collective-permute-start.3 = (f16[4,8192]{1,0:T(4,128)(2,1)S(1)}, f16[4,8192]{1,0:T(4,128)(2,1)S(1)}, u32[]{:S(2)}, u32[]{:S(2)}) collective-permute-start(f16[4,8192]{1,0:T(4,128)(2,1)S(1)} %get-tuple-element.45), channel_id=1, source_target_pairs={{0,2},{1,3},{2,0},{3,1},{4,6},{5,7},{6,4},{7,5},{8,10},{9,11},{10,... | collective-permute-start | bytes 196616 | tf_op jit(solution)/shard_map/ppermute | solution.py:39
  9.6 4.3 %collective-permute-start.2 = (f16[4,8192]{1,0:T(4,128)(2,1)S(1)}, f16[4,8192]{1,0:T(4,128)(2,1)S(1)}, u32[]{:S(2)}, u32[]{:S(2)}) collective-permute-start(f16[4,8192]{1,0:T(4,128)(2,1)S(1)} %get-tuple-element.46), channel_id=1, source_target_pairs={{0,4},{1,5},{2,6},{3,7},{4,0},{5,1},{6,2},{7,3},{8,12},{9,13},{10,... | collective-permute-start | bytes 196616 | tf_op jit(solution)/shard_map/ppermute | solution.py:39
  14.0 5.9 %collective-permute-start.4 = (f16[4,8192]{1,0:T(4,128)(2,1)S(1)}, f16[4,8192]{1,0:T(4,128)(2,1)S(1)}, u32[]{:S(2)}, u32[]{:S(2)}) collective-permute-start(f16[4,8192]{1,0:T(4,128)(2,1)S(1)} %get-tuple-element.40), channel_id=1, source_target_pairs={{0,8},{1,9},{2,10},{3,11},{4,12},{5,13},{6,14},{7,15},{8,0},{9,1},... | collective-permute-start | bytes 196616 | tf_op jit(solution)/shard_map/ppermute | solution.py:39
  20.2 5.6 %collective-permute-start.7 = (bf16[4,8192]{1,0:T(4,128)(2,1)S(1)}, bf16[4,8192]{1,0:T(4,128)(2,1)S(1)}, u32[]{:S(2)}, u32[]{:S(2)}) collective-permute-start(bf16[4,8192]{1,0:T(4,128)(2,1)S(1)} %get-tuple-element.29.refs_1_), channel_id=1, source_target_pairs={{0,6},{1,7},{2,4},{3,5},{4,2},{5,3},{6,0},{7,1},{8,14},{9,15},{10,... | collective-permute-start | bytes 196616 | tf_op jit(solution)/shard_map/ppermute | solution.py:39
  21.0 4.7 %collective-permute-start.6 = (bf16[4,8192]{1,0:T(4,128)(2,1)S(1)}, bf16[4,8192]{1,0:T(4,128)(2,1)S(1)}, u32[]{:S(2)}, u32[]{:S(2)}) collective-permute-start(bf16[4,8192]{1,0:T(4,128)(2,1)S(1)} %get-tuple-element.29.refs_1_), channel_id=1, source_target_pairs={{0,5},{1,4},{2,7},{3,6},{4,1},{5,0},{6,3},{7,2},{8,13},{9,12},{10,... | collective-permute-start | bytes 196616 | tf_op jit(solution)/shard_map/ppermute | solution.py:39
  21.0 5.1 %collective-permute-start.5 = (bf16[4,8192]{1,0:T(4,128)(2,1)S(1)}, bf16[4,8192]{1,0:T(4,128)(2,1)S(1)}, u32[]{:S(2)}, u32[]{:S(2)}) collective-permute-start(bf16[4,8192]{1,0:T(4,128)(2,1)S(1)} %get-tuple-element.29.refs_1_), channel_id=1, source_target_pairs={{0,3},{1,2},{2,1},{3,0},{4,7},{5,6},{6,5},{7,4},{8,11},{9,10},{10,... | collective-permute-start | bytes 196616 | tf_op jit(solution)/shard_map/ppermute | solution.py:39
  26.2 2.0 %collective-permute-start.8 = (bf16[16,8192]{1,0:T(8,128)(2,1)S(1)}, bf16[16,8192]{1,0:T(8,128)(2,1)S(1)}, u32[]{:S(2)}, u32[]{:S(2)}) collective-permute-start(bf16[16,8192]{1,0:T(8,128)(2,1)S(1)} %shard_map.99.refs_2_), channel_id=1, source_target_pairs={{0,1},{1,0},{2,3},{3,2},{4,5},{5,4},{6,7},{7,6},{8,9},{9,8},{10,11... | collective-permute-start | bytes 786440 | tf_op jit(solution)/shard_map/ppermute | solution.py:39
  30.6 1.2 %collective-permute-start.9 = (f32[3,16]{1,0:T(4,128)S(1)}, f32[3,16]{1,0:T(4,128)S(1)}, u32[]{:S(2)}, u32[]{:S(2)}) collective-permute-start(f32[3,16]{1,0:T(4,128)S(1)} %get-tuple-element.31), channel_id=1, source_target_pairs={{0,1},{1,0},{2,3},{3,2},{4,5},{5,4},{6,7},{7,6},{8,9},{9,8},{10,11... | collective-permute-start | bytes 584 | tf_op jit(solution)/shard_map/ppermute | solution.py:39
  31.9 4.5 %collective-permute-start.10 = (f32[3,4]{1,0:T(4,128)S(1)}, f32[3,4]{1,0:T(4,128)S(1)}, u32[]{:S(2)}, u32[]{:S(2)}) collective-permute-start(f32[3,4]{1,0:T(4,128)S(1)} %get-tuple-element.32), channel_id=1, source_target_pairs={{0,6},{1,7},{2,4},{3,5},{4,2},{5,3},{6,0},{7,1},{8,14},{9,15},{10,... | collective-permute-start | bytes 152 | tf_op jit(solution)/shard_map/ppermute | solution.py:39
  32.5 3.9 %collective-permute-start.11 = (f32[3,4]{1,0:T(4,128)S(1)}, f32[3,4]{1,0:T(4,128)S(1)}, u32[]{:S(2)}, u32[]{:S(2)}) collective-permute-start(f32[3,4]{1,0:T(4,128)S(1)} %get-tuple-element.36), channel_id=1, source_target_pairs={{0,3},{1,2},{2,1},{3,0},{4,7},{5,6},{6,5},{7,4},{8,11},{9,10},{10,... | collective-permute-start | bytes 152 | tf_op jit(solution)/shard_map/ppermute | solution.py:39
  33.6 3.0 %collective-permute-start.12 = (f32[3,4]{1,0:T(4,128)S(1)}, f32[3,4]{1,0:T(4,128)S(1)}, u32[]{:S(2)}, u32[]{:S(2)}) collective-permute-start(f32[3,4]{1,0:T(4,128)S(1)} %get-tuple-element.37), channel_id=1, source_target_pairs={{0,5},{1,4},{2,7},{3,6},{4,1},{5,0},{6,3},{7,2},{8,13},{9,12},{10,... | collective-permute-start | bytes 152 | tf_op jit(solution)/shard_map/ppermute | solution.py:39
  36.7 3.9 %collective-permute-start.13 = (f32[3,2]{1,0:T(4,128)S(1)}, f32[3,2]{1,0:T(4,128)S(1)}, u32[]{:S(2)}, u32[]{:S(2)}) collective-permute-start(f32[3,2]{1,0:T(4,128)S(1)} %get-tuple-element.39), channel_id=1, source_target_pairs={{0,9},{1,8},{2,11},{3,10},{4,13},{5,12},{6,15},{7,14},{8,1},{9,0},... | collective-permute-start | bytes 80 | tf_op jit(solution)/shard_map/ppermute | solution.py:39

commit v5 on v4

--- a/solution.py
+++ b/solution.py
@@ -18,13 +18,13 @@
 CHUNKS = 4
 
 
-def levels_of(devices, crossed):
+def levels_of(devices, quad=(0, 0, 0), pair=0):
     levels, stride = [(0, 1)], 2
     while stride < devices:
         if (devices // stride) % 4 == 0:
-            levels.append((0, stride | crossed, 2 * stride | crossed, 3 * stride))
+            levels.append((0, *(k * stride | quad[k - 1] for k in (1, 2, 3))))
         else:
-            levels.append((0, stride | crossed))
+            levels.append((0, stride | pair))
         stride *= len(levels[-1])
     assert stride == devices
     return levels
@@ -196,9 +196,9 @@
     tokens, depth = hidden_units.shape
     vocab_rows = head_weight.shape[0]
     devices = lax.axis_size(AXIS)
-    levels = levels_of(devices, 0)
-    gather_levels = [*levels_of(devices, 1)[:-1], levels_of(devices, 0)[-1]]
-    sum_levels = levels_of(devices, 1)
+    levels = levels_of(devices)
+    gather_levels = [*levels_of(devices, (1, 0, 1))[:-1], levels[-1]]
+    sum_levels = levels_of(devices, (1, 1, 0), 1)
 
     half = (tokens // 2, width)
     gain = final_gain.reshape(-1, 128)

time: 41.5 us -> 40.9 us (0.986)
  waiting for transfers between devices: 11.4 us -> 10.8 us
    ppermute x14, waiting for transfers between devices: 11.4 us -> 10.8 us  [swapped(): lax.ppermute(block, AXIS, [(i, i ^ distance) for i in range(lax.axis_size...]
  transfers between devices with their start and end apart: 14 -> 14, of which waited for: 12 -> 10; matrix products, arithmetic and copies ran while one was open for 0% -> 0% of each run, Pallas kernels for 12% -> 12%
where the time goes in v5:
time: 40.9 us; the launch traced here: 40.7 us
  starting transfers between devices  17.8 us (44%)
  Pallas kernels  11 us (27%)
  waiting for transfers between devices  10.8 us (26%)
  between operations  0.73 us (2%)
    ppermute x14, starting transfers between devices, swapped(): lax.ppermute(block, AXIS, [(i, i ^ distance) for i in range(lax.axis_size...  17.8 us
    pallas_call x10, Pallas kernels, call(): pl.pallas_call(body, out_shape=shapes, in_specs=specs or [WHOLE] * len(op...  11 us
    ppermute x14, waiting for transfers between devices, swapped(): lax.ppermute(block, AXIS, [(i, i ^ distance) for i in range(lax.axis_size...  10.8 us
  transfers between devices with their start and end apart: 14, of which 10 were waited for; matrix products, arithmetic and copies ran while one was open for 0% of the time, Pallas kernels for 12%

profile of v5, /device:TPU:0, one launch (start us, length us, event | category | flops | bytes accessed | tf_op | source)
XLA Modules:
  0.0 40.7 jit_solution(991390338889539853)
XLA Ops:
  0.6 2.6 %shard_map.95 = (f32[16,8192]{1,0:T(8,128)S(1)}, f32[16,8192]{1,0:T(8,128)S(1)}, s32[2,32]{1,0:T(2,128)S(1)}, bf16[2,8192]{1,0:T(2,128)(2,1)S(1)}, bf16[64,128]{...) custom-call(bf16[32,224]{1,0:T(8,128)(2,1)} %refs_0_.1, s32[1,32]{1,0:T(1,128)} %bitcast.6, ...), custom_call_target="tpu_custom_call" | custom-call | tf_op jit(solution)/shard_map/pallas_call | solution.py:48
  3.3 0.5 %collective-permute-start = (f16[16,8192]{1,0:T(8,128)(2,1)S(1)}, f16[16,8192]{1,0:T(8,128)(2,1)S(1)}, u32[]{:S(2)}, u32[]{:S(2)}) collective-permute-start(f16[16,8192]{1,0:T(8,128)(2,1)S(1)} %convert_element_type.27), channel_id=1, source_target_pairs={{0,1},{1,0},{2,3},{3,2},{4,5},{5,4},{6,7},{7,6},{8,9},{9,8},{10,11... | collective-permute-start | bytes 786440 | tf_op jit(solution)/shard_map/ppermute | solution.py:39
  3.8 1.2 %collective-permute-done = f16[16,8192]{1,0:T(8,128)(2,1)S(1)} collective-permute-done((f16[16,8192]{1,0:T(8,128)(2,1)S(1)}, f16[16,8192]{1,0:T(8,128)(2,1)S(1)}, u32[]{:S(2)}, u32[]{:S(2)}) %collective-permute-start) | collective-permute-done | bytes 262176 | tf_op jit(solution)/shard_map/ppermute | solution.py:39
  5.0 0.1 fusion.4
  5.1 4.0 %collective-permute-start.1 = (f16[4,8192]{1,0:T(4,128)(2,1)S(1)}, f16[4,8192]{1,0:T(4,128)(2,1)S(1)}, u32[]{:S(2)}, u32[]{:S(2)}) collective-permute-start(f16[4,8192]{1,0:T(4,128)(2,1)S(1)} %get-tuple-element.44), channel_id=1, source_target_pairs={{0,6},{1,7},{2,4},{3,5},{4,2},{5,3},{6,0},{7,1},{8,14},{9,15},{10,... | collective-permute-start | bytes 196616 | tf_op jit(solution)/shard_map/ppermute | solution.py:39
  9.1 0.5 %collective-permute-start.3 = (f16[4,8192]{1,0:T(4,128)(2,1)S(1)}, f16[4,8192]{1,0:T(4,128)(2,1)S(1)}, u32[]{:S(2)}, u32[]{:S(2)}) collective-permute-start(f16[4,8192]{1,0:T(4,128)(2,1)S(1)} %get-tuple-element.45), channel_id=1, source_target_pairs={{0,2},{1,3},{2,0},{3,1},{4,6},{5,7},{6,4},{7,5},{8,10},{9,11},{10,... | collective-permute-start | bytes 196616 | tf_op jit(solution)/shard_map/ppermute | solution.py:39
  9.6 0.1 collective-permute-start.2
  9.7 1.8 %collective-permute-done.1 = f16[4,8192]{1,0:T(4,128)(2,1)S(1)} collective-permute-done((f16[4,8192]{1,0:T(4,128)(2,1)S(1)}, f16[4,8192]{1,0:T(4,128)(2,1)S(1)}, u32[]{:S(2)}, u32[]{:S(2)}) %collective-permute-start.1) | collective-permute-done | bytes 65568 | tf_op jit(solution)/shard_map/ppermute | solution.py:39
  11.5 1.9 %collective-permute-done.3 = f16[4,8192]{1,0:T(4,128)(2,1)S(1)} collective-permute-done((f16[4,8192]{1,0:T(4,128)(2,1)S(1)}, f16[4,8192]{1,0:T(4,128)(2,1)S(1)}, u32[]{:S(2)}, u32[]{:S(2)}) %collective-permute-start.3) | collective-permute-done | bytes 65568 | tf_op jit(solution)/shard_map/ppermute | solution.py:39
  13.4 0.5 %collective-permute-done.2 = f16[4,8192]{1,0:T(4,128)(2,1)S(1)} collective-permute-done((f16[4,8192]{1,0:T(4,128)(2,1)S(1)}, f16[4,8192]{1,0:T(4,128)(2,1)S(1)}, u32[]{:S(2)}, u32[]{:S(2)}) %collective-permute-start.2) | collective-permute-done | bytes 65568 | tf_op jit(solution)/shard_map/ppermute | solution.py:39
  13.9 0.1 fusion.1
  14.0 2.7 %collective-permute-start.4 = (f16[4,8192]{1,0:T(4,128)(2,1)S(1)}, f16[4,8192]{1,0:T(4,128)(2,1)S(1)}, u32[]{:S(2)}, u32[]{:S(2)}) collective-permute-start(f16[4,8192]{1,0:T(4,128)(2,1)S(1)} %get-tuple-element.40), channel_id=1, source_target_pairs={{0,8},{1,9},{2,10},{3,11},{4,12},{5,13},{6,14},{7,15},{8,0},{9,1},... | collective-permute-start | bytes 196616 | tf_op jit(solution)/shard_map/ppermute | solution.py:39
  16.6 2.2 %shard_map.96.refs_0_ = bf16[256,8192]{1,0:T(8,128)(2,1)S(1)} custom-call(bf16[512,8192]{1,0:T(8,128)(2,1)} %source.3, f32[4,8192]{1,0:T(4,128)S(1)} %get-tuple-element.41.after.mine_ref), custom_call_target="tpu_custom_call" | custom-call | tf_op jit(solution)/shard_map/pallas_call | solution.py:48
  18.8 1.1 %collective-permute-done.4 = f16[4,8192]{1,0:T(4,128)(2,1)S(1)} collective-permute-done((f16[4,8192]{1,0:T(4,128)(2,1)S(1)}, f16[4,8192]{1,0:T(4,128)(2,1)S(1)}, u32[]{:S(2)}, u32[]{:S(2)}) %collective-permute-start.4) | collective-permute-done | bytes 65568 | tf_op jit(solution)/shard_map/ppermute | solution.py:39
  19.9 0.3 shard_map.97
  20.3 0.3 collective-permute-start.6
  20.6 2.6 %collective-permute-start.5 = (bf16[4,8192]{1,0:T(4,128)(2,1)S(1)}, bf16[4,8192]{1,0:T(4,128)(2,1)S(1)}, u32[]{:S(2)}, u32[]{:S(2)}) collective-permute-start(bf16[4,8192]{1,0:T(4,128)(2,1)S(1)} %get-tuple-element.29.refs_1_), channel_id=1, source_target_pairs={{0,3},{1,2},{2,1},{3,0},{4,7},{5,6},{6,5},{7,4},{8,11},{9,10},{10,... | collective-permute-start | bytes 196616 | tf_op jit(solution)/shard_map/ppermute | solution.py:39
  23.2 2.2 %shard_map.98.refs_0_.refs_1_ = bf16[256,8192]{1,0:T(8,128)(2,1)S(1)} custom-call(bf16[512,8192]{1,0:T(8,128)(2,1)} %source.3, bf16[2,8192]{1,0:T(2,128)(2,1)S(1)} %get-tuple-element.26.after.source), custom_call_target="tpu_custom_call" | custom-call | tf_op jit(solution)/shard_map/pallas_call | solution.py:48
  25.4 0.1 collective-permute-done.5.refs_2_
  25.6 1.2 %collective-permute-start.8 = (bf16[16,8192]{1,0:T(8,128)(2,1)S(1)}, bf16[16,8192]{1,0:T(8,128)(2,1)S(1)}, u32[]{:S(2)}, u32[]{:S(2)}) collective-permute-start(bf16[16,8192]{1,0:T(8,128)(2,1)S(1)} %shard_map.99.refs_2_), channel_id=1, source_target_pairs={{0,1},{1,0},{2,3},{3,2},{4,5},{5,4},{6,7},{7,6},{8,9},{9,8},{10,11... | collective-permute-start | bytes 786440 | tf_op jit(solution)/shard_map/ppermute | solution.py:39
  26.8 1.2 %collective-permute-done.8.refs_3_ = bf16[16,8192]{1,0:T(8,128)(2,1)S(1)} collective-permute-done((bf16[16,8192]{1,0:T(8,128)(2,1)S(1)}, bf16[16,8192]{1,0:T(8,128)(2,1)S(1)}, u32[]{:S(2)}, u32[]{:S(2)}) %collective-permute-start.8) | collective-permute-done | bytes 262176 | tf_op jit(solution)/shard_map/ppermute | solution.py:39
  28.0 2.4 %shard_map.100 = (f32[3,16]{1,0:T(4,128)S(1)}, f32[3,16]{1,0:T(4,128)S(1)}) custom-call(s32[2,32]{1,0:T(2,128)S(1)} %get-tuple-element.27.facts_ref, bf16[256,8192]{1,0:T(8,128)(2,1)S(1)} %shard_map.96.refs_0_, bf16[256,8192]{1,0:T(8,128)(2,1)S(1)} %shard_map.98.refs_0_.refs_1_, bf16[16,8192]{1,0:T(8,128)(2,1)S(1)} %shard_map.99.refs_2_, ...), custom_call_target="tpu_custom_call" | custom-call | tf_op jit(solution)/shard_map/pallas_call | solution.py:48
  30.3 0.4 collective-permute-start.9
  30.7 0.8 %collective-permute-done.9.refs_0_ = f32[3,16]{1,0:T(4,128)S(1)} collective-permute-done((f32[3,16]{1,0:T(4,128)S(1)}, f32[3,16]{1,0:T(4,128)S(1)}, u32[]{:S(2)}, u32[]{:S(2)}) %collective-permute-start.9) | collective-permute-done | bytes 224 | tf_op jit(solution)/shard_map/ppermute | solution.py:39
  31.6 1.1 %collective-permute-start.10 = (f32[3,4]{1,0:T(4,128)S(1)}, f32[3,4]{1,0:T(4,128)S(1)}, u32[]{:S(2)}, u32[]{:S(2)}) collective-permute-start(f32[3,4]{1,0:T(4,128)S(1)} %get-tuple-element.32), channel_id=1, source_target_pairs={{0,6},{1,7},{2,4},{3,5},{4,2},{5,3},{6,0},{7,1},{8,14},{9,15},{10,... | collective-permute-start | bytes 152 | tf_op jit(solution)/shard_map/ppermute | solution.py:39
  32.7 0.3 collective-permute-start.11
  33.0 1.8 %collective-permute-start.12 = (f32[3,4]{1,0:T(4,128)S(1)}, f32[3,4]{1,0:T(4,128)S(1)}, u32[]{:S(2)}, u32[]{:S(2)}) collective-permute-start(f32[3,4]{1,0:T(4,128)S(1)} %get-tuple-element.37), channel_id=1, source_target_pairs={{0,5},{1,4},{2,7},{3,6},{4,1},{5,0},{6,3},{7,2},{8,13},{9,12},{10,... | collective-permute-start | bytes 152 | tf_op jit(solution)/shard_map/ppermute | solution.py:39
  34.8 1.3 %collective-permute-done.10.after.refs_0_ = f32[3,4]{1,0:T(4,128)S(1)} collective-permute-done((f32[3,4]{1,0:T(4,128)S(1)}, f32[3,4]{1,0:T(4,128)S(1)}, u32[]{:S(2)}, u32[]{:S(2)}) %collective-permute-start.10) | collective-permute-done | bytes 80 | tf_op jit(solution)/shard_map/ppermute | solution.py:39
  36.2 2.3 %collective-permute-start.13 = (f32[3,2]{1,0:T(4,128)S(1)}, f32[3,2]{1,0:T(4,128)S(1)}, u32[]{:S(2)}, u32[]{:S(2)}) collective-permute-start(f32[3,2]{1,0:T(4,128)S(1)} %get-tuple-element.39), channel_id=1, source_target_pairs={{0,9},{1,8},{2,11},{3,10},{4,13},{5,12},{6,15},{7,14},{8,1},{9,0},... | collective-permute-start | bytes 80 | tf_op jit(solution)/shard_map/ppermute | solution.py:39
  38.5 0.6 %shard_map.102 = bf16[2,8192]{1,0:T(2,128)(2,1)} custom-call(bf16[2,8192]{1,0:T(2,128)(2,1)S(1)} %get-tuple-element.26.after.source, f32[3,4]{1,0:T(4,128)S(1)} %collective-permute-done.10.after.refs_0_), custom_call_target="tpu_custom_call" | custom-call | tf_op jit(solution)/shard_map/pallas_call | solution.py:48
  39.2 1.0 %collective-permute-done.13.refs_0_ = f32[3,2]{1,0:T(4,128)S(1)} collective-permute-done((f32[3,2]{1,0:T(4,128)S(1)}, f32[3,2]{1,0:T(4,128)S(1)}, u32[]{:S(2)}, u32[]{:S(2)}) %collective-permute-start.13) | collective-permute-done | bytes 56 | tf_op jit(solution)/shard_map/ppermute | solution.py:39
  40.1 0.5 %shard_map.104 = f32[1,2]{1,0:T(1,128)} custom-call(s32[1,2]{1,0:T(1,128)S(1)} %get-tuple-element.33.segments_ref, f32[1,2]{1,0:T(1,128)S(1)} %get-tuple-element.34.train_ref, f32[3,2]{1,0:T(4,128)S(1)} %get-tuple-element.38.keep_ref, f32[3,2]{1,0:T(4,128)S(1)} %collective-permute-done.13.refs_0_), custom_call_target="tpu_custom_call" | custom-call | tf_op jit(solution)/shard_map/pallas_call | solution.py:48
  (11 shorter events, 0.4 us)
Async XLA Ops:
  3.3 1.7 %collective-permute-start = (f16[16,8192]{1,0:T(8,128)(2,1)S(1)}, f16[16,8192]{1,0:T(8,128)(2,1)S(1)}, u32[]{:S(2)}, u32[]{:S(2)}) collective-permute-start(f16[16,8192]{1,0:T(8,128)(2,1)S(1)} %convert_element_type.27), channel_id=1, source_target_pairs={{0,1},{1,0},{2,3},{3,2},{4,5},{5,4},{6,7},{7,6},{8,9},{9,8},{10,11... | collective-permute-start | bytes 786440 | tf_op jit(solution)/shard_map/ppermute | solution.py:39
  5.1 6.4 %collective-permute-start.1 = (f16[4,8192]{1,0:T(4,128)(2,1)S(1)}, f16[4,8192]{1,0:T(4,128)(2,1)S(1)}, u32[]{:S(2)}, u32[]{:S(2)}) collective-permute-start(f16[4,8192]{1,0:T(4,128)(2,1)S(1)} %get-tuple-element.44), channel_id=1, source_target_pairs={{0,6},{1,7},{2,4},{3,5},{4,2},{5,3},{6,0},{7,1},{8,14},{9,15},{10,... | collective-permute-start | bytes 196616 | tf_op jit(solution)/shard_map/ppermute | solution.py:39
  9.1 4.3 %collective-permute-start.3 = (f16[4,8192]{1,0:T(4,128)(2,1)S(1)}, f16[4,8192]{1,0:T(4,128)(2,1)S(1)}, u32[]{:S(2)}, u32[]{:S(2)}) collective-permute-start(f16[4,8192]{1,0:T(4,128)(2,1)S(1)} %get-tuple-element.45), channel_id=1, source_target_pairs={{0,2},{1,3},{2,0},{3,1},{4,6},{5,7},{6,4},{7,5},{8,10},{9,11},{10,... | collective-permute-start | bytes 196616 | tf_op jit(solution)/shard_map/ppermute | solution.py:39
  9.6 4.3 %collective-permute-start.2 = (f16[4,8192]{1,0:T(4,128)(2,1)S(1)}, f16[4,8192]{1,0:T(4,128)(2,1)S(1)}, u32[]{:S(2)}, u32[]{:S(2)}) collective-permute-start(f16[4,8192]{1,0:T(4,128)(2,1)S(1)} %get-tuple-element.46), channel_id=1, source_target_pairs={{0,4},{1,5},{2,6},{3,7},{4,0},{5,1},{6,2},{7,3},{8,12},{9,13},{10,... | collective-permute-start | bytes 196616 | tf_op jit(solution)/shard_map/ppermute | solution.py:39
  14.0 5.9 %collective-permute-start.4 = (f16[4,8192]{1,0:T(4,128)(2,1)S(1)}, f16[4,8192]{1,0:T(4,128)(2,1)S(1)}, u32[]{:S(2)}, u32[]{:S(2)}) collective-permute-start(f16[4,8192]{1,0:T(4,128)(2,1)S(1)} %get-tuple-element.40), channel_id=1, source_target_pairs={{0,8},{1,9},{2,10},{3,11},{4,12},{5,13},{6,14},{7,15},{8,0},{9,1},... | collective-permute-start | bytes 196616 | tf_op jit(solution)/shard_map/ppermute | solution.py:39
  20.2 5.2 %collective-permute-start.7 = (bf16[4,8192]{1,0:T(4,128)(2,1)S(1)}, bf16[4,8192]{1,0:T(4,128)(2,1)S(1)}, u32[]{:S(2)}, u32[]{:S(2)}) collective-permute-start(bf16[4,8192]{1,0:T(4,128)(2,1)S(1)} %get-tuple-element.29.refs_1_), channel_id=1, source_target_pairs={{0,7},{1,6},{2,5},{3,4},{4,3},{5,2},{6,1},{7,0},{8,15},{9,14},{10,... | collective-permute-start | bytes 196616 | tf_op jit(solution)/shard_map/ppermute | solution.py:39
  20.3 5.1 %collective-permute-start.6 = (bf16[4,8192]{1,0:T(4,128)(2,1)S(1)}, bf16[4,8192]{1,0:T(4,128)(2,1)S(1)}, u32[]{:S(2)}, u32[]{:S(2)}) collective-permute-start(bf16[4,8192]{1,0:T(4,128)(2,1)S(1)} %get-tuple-element.29.refs_1_), channel_id=1, source_target_pairs={{0,4},{1,5},{2,6},{3,7},{4,0},{5,1},{6,2},{7,3},{8,12},{9,13},{10,... | collective-permute-start | bytes 196616 | tf_op jit(solution)/shard_map/ppermute | solution.py:39
  20.6 5.0 %collective-permute-start.5 = (bf16[4,8192]{1,0:T(4,128)(2,1)S(1)}, bf16[4,8192]{1,0:T(4,128)(2,1)S(1)}, u32[]{:S(2)}, u32[]{:S(2)}) collective-permute-start(bf16[4,8192]{1,0:T(4,128)(2,1)S(1)} %get-tuple-element.29.refs_1_), channel_id=1, source_target_pairs={{0,3},{1,2},{2,1},{3,0},{4,7},{5,6},{6,5},{7,4},{8,11},{9,10},{10,... | collective-permute-start | bytes 196616 | tf_op jit(solution)/shard_map/ppermute | solution.py:39
  25.6 2.3 %collective-permute-start.8 = (bf16[16,8192]{1,0:T(8,128)(2,1)S(1)}, bf16[16,8192]{1,0:T(8,128)(2,1)S(1)}, u32[]{:S(2)}, u32[]{:S(2)}) collective-permute-start(bf16[16,8192]{1,0:T(8,128)(2,1)S(1)} %shard_map.99.refs_2_), channel_id=1, source_target_pairs={{0,1},{1,0},{2,3},{3,2},{4,5},{5,4},{6,7},{7,6},{8,9},{9,8},{10,11... | collective-permute-start | bytes 786440 | tf_op jit(solution)/shard_map/ppermute | solution.py:39
  30.3 1.2 %collective-permute-start.9 = (f32[3,16]{1,0:T(4,128)S(1)}, f32[3,16]{1,0:T(4,128)S(1)}, u32[]{:S(2)}, u32[]{:S(2)}) collective-permute-start(f32[3,16]{1,0:T(4,128)S(1)} %get-tuple-element.31), channel_id=1, source_target_pairs={{0,1},{1,0},{2,3},{3,2},{4,5},{5,4},{6,7},{7,6},{8,9},{9,8},{10,11... | collective-permute-start | bytes 584 | tf_op jit(solution)/shard_map/ppermute | solution.py:39
  31.6 4.5 %collective-permute-start.10 = (f32[3,4]{1,0:T(4,128)S(1)}, f32[3,4]{1,0:T(4,128)S(1)}, u32[]{:S(2)}, u32[]{:S(2)}) collective-permute-start(f32[3,4]{1,0:T(4,128)S(1)} %get-tuple-element.32), channel_id=1, source_target_pairs={{0,6},{1,7},{2,4},{3,5},{4,2},{5,3},{6,0},{7,1},{8,14},{9,15},{10,... | collective-permute-start | bytes 152 | tf_op jit(solution)/shard_map/ppermute | solution.py:39
  32.7 3.4 %collective-permute-start.11 = (f32[3,4]{1,0:T(4,128)S(1)}, f32[3,4]{1,0:T(4,128)S(1)}, u32[]{:S(2)}, u32[]{:S(2)}) collective-permute-start(f32[3,4]{1,0:T(4,128)S(1)} %get-tuple-element.36), channel_id=1, source_target_pairs={{0,3},{1,2},{2,1},{3,0},{4,7},{5,6},{6,5},{7,4},{8,11},{9,10},{10,... | collective-permute-start | bytes 152 | tf_op jit(solution)/shard_map/ppermute | solution.py:39
  33.0 3.1 %collective-permute-start.12 = (f32[3,4]{1,0:T(4,128)S(1)}, f32[3,4]{1,0:T(4,128)S(1)}, u32[]{:S(2)}, u32[]{:S(2)}) collective-permute-start(f32[3,4]{1,0:T(4,128)S(1)} %get-tuple-element.37), channel_id=1, source_target_pairs={{0,5},{1,4},{2,7},{3,6},{4,1},{5,0},{6,3},{7,2},{8,13},{9,12},{10,... | collective-permute-start | bytes 152 | tf_op jit(solution)/shard_map/ppermute | solution.py:39
  36.2 3.9 %collective-permute-start.13 = (f32[3,2]{1,0:T(4,128)S(1)}, f32[3,2]{1,0:T(4,128)S(1)}, u32[]{:S(2)}, u32[]{:S(2)}) collective-permute-start(f32[3,2]{1,0:T(4,128)S(1)} %get-tuple-element.39), channel_id=1, source_target_pairs={{0,9},{1,8},{2,11},{3,10},{4,13},{5,12},{6,15},{7,14},{8,1},{9,0},... | collective-permute-start | bytes 80 | tf_op jit(solution)/shard_map/ppermute | solution.py:39
